TPU v7x, 512 devices: a whole 4x4x16 slice. The times are simulated.
512 devices in a mesh: section: 8 (over y, core), peer: 64 (over x, z).
Axes of the slice: x: 4, y: 4, z: 16, core: 2. Of those that a mesh axis runs over, the one named last changes fastest.
Arguments:
- pending_activations: bfloat16 [8, 128, 2560], P('section', 'peer'), may hold values from -6 to 6
- new_first_inputs: bfloat16 [1, 128, 2560], P(None, 'peer'), may hold values from -6 to 6
- stored_section_inputs: bfloat16 [2, 8, 128, 2560], P(None, 'section', 'peer'), may hold values from -6 to 6
- pending_gradients: bfloat16 [8, 128, 2560], P('section', 'peer'), may hold values from -1.5 to 1.5
- loss_gradients: bfloat16 [1, 128, 2560], P(None, 'peer'), may hold values from -1.5 to 1.5
- forward_wiring: int32 [2, 8, 128], replicated, may hold values from 0 to 127, each once within a row
- backward_wiring: int32 [2, 8, 128], replicated, may hold values from 0 to 127, each once within a row
- norm_gain_vector: float32 [8, 2560], P('section'), may hold values from 0.25 to 1.75
- up_projection_weight: bfloat16 [8, 10240, 2560], P('section', 'peer'), may hold values from -0.125 to 0.125
- down_projection_weight: bfloat16 [8, 10240, 2560], P('section', 'peer'), may hold values from -0.0625 to 0.0625
Outputs:
- section_outputs: bfloat16 [2, 8, 128, 2560], P(None, 'section', 'peer')
- input_grads: bfloat16 [2, 8, 128, 2560], P(None, 'section', 'peer')
- up_grad: bfloat16 [8, 10240, 2560], P('section', 'peer')
- down_grad: bfloat16 [8, 10240, 2560], P('section', 'peer')
- gain_grad: float32 [8, 2560], P('section')
Inputs may be any that keep to these rules, and one draw needn't show every extreme that they name: Each row of forward_wiring[k, s] names every received row once. Each row of backward_wiring[k, s] names every arrival position once.
All inputs are finite; a program needn't handle non-finite values.
Results may differ from a plain program's by a relative error of at most 0.007.
Values may be sent and summed in bfloat16 or wider, within the bound.
A program may use at most 64 MiB of HBM per device.

v0:
```python
import jax
import jax.numpy as jnp
from jax import lax
from jax.sharding import PartitionSpec as P

epsilon = 1e-05


def swapped(block, axis, stride):
    count = lax.axis_size(axis)
    route = []
    for low in range(count):
        high = low | 1 << stride
        if high != low and high < count:
            route += [(low, high), (high, low)]
    return lax.ppermute(block, axis, route)


def passed_along(block, axis, distance):
    devices = range(lax.axis_size(axis))
    route = [(i - distance, i) for i in devices if i - distance in devices]
    return lax.ppermute(block, axis, route)


def norm_parts(x, gain_row):
    as_float = x.astype(jnp.float32)
    inv_rms = lax.rsqrt(jnp.mean(as_float * as_float, axis=-1, keepdims=True) + epsilon)
    normed = (as_float * inv_rms * gain_row).astype(jnp.bfloat16)
    return (as_float, inv_rms, normed)


def up_project(normed, up_mat):
    return lax.dot_general(
        normed, up_mat, (((1,), (1,)), ((), ())), preferred_element_type=jnp.float32
    )


def inverse_order(route):
    count = route.shape[0]
    return jnp.zeros((count,), jnp.int32).at[route].set(jnp.arange(count, dtype=jnp.int32))


def bit_of(value, bit):
    return value // (1 << bit) % 2 == 1


def halve_sum(block, group_id, group_bits):
    for bit in reversed(range(group_bits)):
        half = block.shape[0] // 2
        upper_bit = bit_of(group_id, bit)
        first_half = block[:half]
        second_half = block[half:]
        keep = jnp.where(upper_bit, second_half, first_half)
        sending = jnp.where(upper_bit, first_half, second_half)
        block = keep + swapped(sending, "peer", bit)
    return block


def double_rows(pieces, group_id, group_bits):
    for bit in range(group_bits):
        upper_bit = bit_of(group_id, bit)
        got = swapped((pieces[0], pieces[1]), "peer", bit)
        pieces = tuple(
            (
                jnp.where(
                    upper_bit,
                    jnp.concatenate([other, mine], axis=0),
                    jnp.concatenate([mine, other], axis=0),
                )
                for mine, other in zip(pieces, got)
            )
        )
    return pieces


def on_device(
    pending_activations,
    new_first_inputs,
    stored_section_inputs,
    pending_gradients,
    loss_gradients,
    forward_wiring,
    backward_wiring,
    norm_gain_vector,
    up_projection_weight,
    down_projection_weight,
):
    section_id = lax.axis_index("section")
    peer_id = lax.axis_index("peer")
    section_count = lax.axis_size("section")
    peer_count = lax.axis_size("peer")
    local_rows = pending_activations.shape[1]
    model_feature_width = pending_activations.shape[2]
    tick_count = forward_wiring.shape[0]
    is_first = section_id == 0
    is_last = section_id == section_count - 1
    gain_row = norm_gain_vector[0]
    up_own = up_projection_weight[0]
    down_own = down_projection_weight[0]
    shard_units = up_own.shape[0]
    peer_bits = peer_count.bit_length() - 1
    group_bits = peer_bits - 1
    replica_id = peer_id // (1 << group_bits)
    group_id = peer_id - replica_id * (1 << group_bits)
    lower_first = replica_id == 0
    got_up, got_down = swapped((up_own, down_own), "peer", group_bits)
    up_local = jnp.where(
        lower_first,
        jnp.concatenate([up_own, got_up], axis=0),
        jnp.concatenate([got_up, up_own], axis=0),
    )
    down_local = jnp.where(
        lower_first,
        jnp.concatenate([down_own, got_down], axis=0),
        jnp.concatenate([got_down, down_own], axis=0),
    )
    group_rows = local_rows * (1 << group_bits)
    group_start = replica_id * group_rows
    local_start = group_id * local_rows
    gain_total = jnp.zeros((model_feature_width,), jnp.float32)
    out_rows = []
    grad_rows = []
    normed_steps = []
    d_pre_steps = []
    hidden_steps = []
    grad_steps = []
    prev_out = None
    prev_grad = None
    for moment in range(tick_count):
        row_order = lax.dynamic_index_in_dim(forward_wiring[moment], section_id, 0, keepdims=False)
        if moment == 0:
            input_rows = pending_activations[0]
        else:
            input_rows = jnp.where(
                is_first, new_first_inputs[moment - 1], passed_along(prev_out, "section", 1)
            )
        whole_in = lax.all_gather(input_rows, "peer", axis=0, tiled=True)
        group_order = lax.dynamic_slice_in_dim(row_order, group_start, group_rows, 0)
        used = jnp.take(whole_in, group_order, axis=0)
        as_float, inv_rms, normed = norm_parts(used, gain_row)
        hidden = jax.nn.silu(up_project(normed, up_local)).astype(jnp.bfloat16)
        branch = jnp.dot(hidden, down_local, preferred_element_type=jnp.float32)
        summed = halve_sum(branch, group_id, group_bits)
        own_float = lax.dynamic_slice_in_dim(as_float, local_start, local_rows, 0)
        prev_out = (own_float + summed).astype(jnp.bfloat16)
        out_rows.append(prev_out)
        if moment == 0:
            gradient_input_rows = pending_gradients[0]
        else:
            gradient_input_rows = jnp.where(
                is_last, loss_gradients[moment - 1], passed_along(prev_grad, "section", -1)
            )
        saved_group, grad_group = double_rows(
            (stored_section_inputs[moment, 0], gradient_input_rows), group_id, group_bits
        )
        as_float, inv_rms, normed = norm_parts(saved_group, gain_row)
        pre_act = up_project(normed, up_local)
        hidden = jax.nn.silu(pre_act).astype(jnp.bfloat16)
        d_hidden = lax.dot_general(
            grad_group, down_local, (((1,), (1,)), ((), ())), preferred_element_type=jnp.float32
        )
        sigma = jax.nn.sigmoid(pre_act)
        d_pre = (d_hidden * sigma * (1.0 + pre_act * (1.0 - sigma))).astype(jnp.bfloat16)
        normed_steps.append(normed)
        d_pre_steps.append(d_pre)
        hidden_steps.append(hidden)
        grad_steps.append(grad_group)
        d_normed = jnp.dot(d_pre, up_local, preferred_element_type=jnp.float32)
        d_norm_own = halve_sum(d_normed, group_id, group_bits)
        x_own = lax.dynamic_slice_in_dim(as_float, local_start, local_rows, 0)
        rms_own = lax.dynamic_slice_in_dim(inv_rms, local_start, local_rows, 0)
        grad_own = gradient_input_rows.astype(jnp.float32)
        gain_part = jnp.sum(d_norm_own * x_own * rms_own, axis=0)
        scaled = d_norm_own * gain_row
        cube = rms_own * rms_own * rms_own
        d_input = rms_own * scaled - x_own * cube * jnp.mean(scaled * x_own, axis=-1, keepdims=True)
        d_rounded = (grad_own + d_input).astype(jnp.bfloat16)
        gathered = lax.all_gather(d_rounded, "peer", axis=0, tiled=True)
        back_order = inverse_order(
            lax.dynamic_index_in_dim(backward_wiring[moment], section_id, 0, keepdims=False)
        )
        own_index = lax.dynamic_slice_in_dim(back_order, peer_id * local_rows, local_rows, 0)
        prev_grad = jnp.take(gathered, own_index, axis=0)
        grad_rows.append(prev_grad)
        gain_total = gain_total + lax.psum(gain_part, "peer")
    all_normed = jnp.concatenate(normed_steps, axis=0)
    all_d_pre = jnp.concatenate(d_pre_steps, axis=0)
    all_hidden = jnp.concatenate(hidden_steps, axis=0)
    all_grad = jnp.concatenate(grad_steps, axis=0)
    acc_up = lax.dot_general(
        all_d_pre, all_normed, (((0,), (0,)), ((), ())), preferred_element_type=jnp.float32
    )
    acc_down = lax.dot_general(
        all_hidden, all_grad, (((0,), (0,)), ((), ())), preferred_element_type=jnp.float32
    )
    keep_up = jnp.where(lower_first, acc_up[:shard_units], acc_up[shard_units:])
    send_up = jnp.where(lower_first, acc_up[shard_units:], acc_up[:shard_units])
    keep_down = jnp.where(lower_first, acc_down[:shard_units], acc_down[shard_units:])
    send_down = jnp.where(lower_first, acc_down[shard_units:], acc_down[:shard_units])
    got_up_grad, got_down_grad = swapped((send_up, send_down), "peer", group_bits)
    up_final = (keep_up + got_up_grad) * 0.5
    down_final = (keep_down + got_down_grad) * 0.5
    section_outputs = jnp.stack(out_rows)[:, None]
    input_grads = jnp.stack(grad_rows)[:, None]
    return (
        section_outputs,
        input_grads,
        up_final.astype(jnp.bfloat16)[None],
        down_final.astype(jnp.bfloat16)[None],
        gain_total[None],
    )


def solution(mesh):
    placed = (
        P("section", "peer", None),
        P(None, "peer", None),
        P(None, "section", "peer", None),
        P("section", "peer", None),
        P(None, "peer", None),
        P(),
        P(),
        P("section", None),
        P("section", "peer", None),
        P("section", "peer", None),
    )
    return jax.shard_map(
        on_device,
        mesh=mesh,
        in_specs=placed,
        out_specs=(
            P(None, "section", "peer", None),
            P(None, "section", "peer", None),
            P("section", "peer", None),
            P("section", "peer", None),
            P("section", None),
        ),
        check_vma=False,
    )
```

profile of v0, /device:TPU:16, one launch (start us, length us, event | category | flops | bytes accessed | tf_op | source)
XLA Modules:
  0.0 1045.8 jit_solution(10052840085036174688)
XLA Ops:
  11.1 4.9 collective-permute-start
  20.0 131.8 %all-gather = bf16[1,128,2560]{2,0,1:T(2,128)(2,1)S(1)} all-gather(bf16[1,2,2560]{2,0,1:T(2,128)(2,1)S(1)} %copy.20), channel_id=2, replica_groups=mesh['section'=8,'peer'=64] {'peer'}, dimensions={1}, use_global_device_ids=true | all-gather | bytes 665600 | tf_op jit(solution)/shard_map/all_gather | solution.py:137
  167.8 5.8 collective-permute-start.20
  177.7 5.8 collective-permute-start.15
  186.6 8.4 collective-permute-start.32
  195.1 6.1 collective-permute-start.21
  201.3 8.4 collective-permute-start.16
  246.8 10.2 collective-permute-start.24
  265.0 9.5 collective-permute-done.3
  278.8 4.7 collective-permute-start.26
  286.8 7.6 collective-permute-start.27
  299.0 100.8 %all-gather.2 = bf16[64,2,2560]{2,1,0:T(2,128)(2,1)S(1)} all-gather(bf16[1,2,2560]{2,1,0:T(2,128)(2,1)S(1)} %fusion.35), channel_id=1, replica_groups=mesh['section'=8,'peer'=64] {'peer'}, dimensions={0}, use_global_device_ids=true | all-gather | bytes 665600 | tf_op jit(solution)/shard_map/all_gather | solution.py:178
  409.5 98.3 %all-gather.1 = bf16[64,2,2560]{2,1,0:T(2,128)(2,1)S(1)} all-gather(bf16[1,2,2560]{2,1,0:T(2,128)(2,1)S(1)} %fusion.32), channel_id=1, replica_groups=mesh['section'=8,'peer'=64] {'peer'}, dimensions={0}, use_global_device_ids=true | all-gather | bytes 665600 | tf_op jit(solution)/shard_map/all_gather | solution.py:137
  517.5 5.8 collective-permute-start.36
  527.6 7.5 collective-permute-start.37
  564.3 7.3 collective-permute-start.9
  572.3 10.8 %collective-permute-done.9 = f32[16,2560]{1,0:T(8,128)S(1)} collective-permute-done((f32[16,2560]{1,0:T(8,128)S(1)}, f32[16,2560]{1,0:T(8,128)S(1)}, u32[]{:S(2)}, u32[]{:S(2)}) %collective-permute-start.9) | collective-permute-done | bytes 163872 | tf_op jit(solution)/shard_map/ppermute | solution.py:16
  583.1 14.7 %collective-permute-start.10 = (f32[8,2560]{1,0:T(8,128)S(1)}, f32[8,2560]{1,0:T(8,128)S(1)}, u32[]{:S(2)}, u32[]{:S(2)}) collective-permute-start(f32[8,2560]{1,0:T(8,128)S(1)} %slice_select_fusion.12), channel_id=1, source_target_pairs={{0,4},{4,0},{1,5},{5,1},{2,6},{6,2},{3,7},{7,3},{8,12},{12,8},{9,1... | collective-permute-start | bytes 245768 | tf_op jit(solution)/shard_map/ppermute | solution.py:16
  606.8 7.2 collective-permute-start.40
  614.1 12.4 %collective-permute-done.40 = f32[16,2560]{1,0:T(8,128)S(1)} collective-permute-done((f32[16,2560]{1,0:T(8,128)S(1)}, f32[16,2560]{1,0:T(8,128)S(1)}, u32[]{:S(2)}, u32[]{:S(2)}) %collective-permute-start.40) | collective-permute-done | bytes 163872 | tf_op jit(solution)/shard_map/ppermute | solution.py:16
  628.5 8.1 collective-permute-start.12
  637.5 5.4 collective-permute-start.42
  651.8 275.8 %psum.16 = f32[2560]{0:T(1024)S(1)} all-reduce(f32[2560]{0:T(1024)S(1)} %add.300), channel_id=1, replica_groups=mesh['section'=8,'peer'=64] {'peer'}, use_global_device_ids=true, to_apply=%region_9.12 | all-reduce | flops 2560 | bytes 20480 | tf_op jit(solution)/shard_map/psum | solution.py:185
  929.2 105.7 %all-gather.3 = bf16[64,2,2560]{2,1,0:T(2,128)(2,1)} all-gather(bf16[1,2,2560]{2,1,0:T(2,128)(2,1)S(1)} %fusion.36), channel_id=1, replica_groups=mesh['section'=8,'peer'=64] {'peer'}, dimensions={0}, use_global_device_ids=true | all-gather | bytes 665600 | tf_op jit(solution)/shard_map/all_gather | solution.py:178
  (261 shorter events, 180.2 us)
Async XLA Ops:
  0.6 160.2 %collective-permute-start.18 = (bf16[2,2560]{1,0:T(2,128)(2,1)}, bf16[2,2560]{1,0:T(2,128)(2,1)S(1)}, u32[]{:S(2)}, u32[]{:S(2)}) collective-permute-start(bf16[2,2560]{1,0:T(2,128)(2,1)} %bitcast.92), channel_id=1, source_target_pairs={{0,1},{1,0},{2,3},{3,2},{4,5},{5,4},{6,7},{7,6},{8,9},{9,8},{10,11... | collective-permute-start | bytes 30728 | tf_op jit(solution)/shard_map/ppermute | solution.py:16
  5.2 160.3 %collective-permute-start.13 = (bf16[2,2560]{1,0:T(2,128)(2,1)S(1)}, bf16[2,2560]{1,0:T(2,128)(2,1)S(1)}, u32[]{:S(2)}, u32[]{:S(2)}) collective-permute-start(bf16[2,2560]{1,0:T(2,128)(2,1)S(1)} %get-tuple-element.40), channel_id=1, source_target_pairs={{0,1},{1,0},{2,3},{3,2},{4,5},{5,4},{6,7},{7,6},{8,9},{9,8},{10,11... | collective-permute-start | bytes 30728 | tf_op jit(solution)/shard_map/ppermute | solution.py:16
  7.2 151.4 %collective-permute-start.29 = (bf16[2,2560]{1,0:T(2,128)(2,1)S(1)}, bf16[2,2560]{1,0:T(2,128)(2,1)S(1)}, u32[]{:S(2)}, u32[]{:S(2)}) collective-permute-start(bf16[2,2560]{1,0:T(2,128)(2,1)S(1)} %get-tuple-element.41), channel_id=1, source_target_pairs={{0,1},{1,0},{2,3},{3,2},{4,5},{5,4},{6,7},{7,6},{8,9},{9,8},{10,11... | collective-permute-start | bytes 30728 | tf_op jit(solution)/shard_map/ppermute | solution.py:16
  11.1 218.0 %collective-permute-start = (bf16[160,2560]{1,0:T(8,128)(2,1)}, bf16[160,2560]{1,0:T(8,128)(2,1)S(1)}, u32[]{:S(2)}, u32[]{:S(2)}) collective-permute-start(bf16[160,2560]{1,0:T(8,128)(2,1)} %bitcast.89), channel_id=1, source_target_pairs={{0,32},{32,0},{1,33},{33,1},{2,34},{34,2},{3,35},{35,3},{4,36},{36... | collective-permute-start | bytes 2457608 | tf_op jit(solution)/shard_map/ppermute | solution.py:16
  16.0 214.2 %collective-permute-start.1 = (bf16[160,2560]{1,0:T(8,128)(2,1)}, bf16[160,2560]{1,0:T(8,128)(2,1)}, u32[]{:S(2)}, u32[]{:S(2)}) collective-permute-start(bf16[160,2560]{1,0:T(8,128)(2,1)} %bitcast.94), channel_id=1, source_target_pairs={{0,32},{32,0},{1,33},{33,1},{2,34},{34,2},{3,35},{35,3},{4,36},{36... | collective-permute-start | bytes 2457608 | tf_op jit(solution)/shard_map/ppermute | solution.py:16
  158.7 14.9 %collective-permute-start.30 = (bf16[4,2560]{1,0:T(4,128)(2,1)S(1)}, bf16[4,2560]{1,0:T(4,128)(2,1)S(1)}, u32[]{:S(2)}, u32[]{:S(2)}) collective-permute-start(bf16[4,2560]{1,0:T(4,128)(2,1)S(1)} %maximum_select_fusion.20), channel_id=1, source_target_pairs={{0,2},{2,0},{1,3},{3,1},{4,6},{6,4},{5,7},{7,5},{8,10},{10,8},{9,1... | collective-permute-start | bytes 61448 | tf_op jit(solution)/shard_map/ppermute | solution.py:16
  167.8 27.3 %collective-permute-start.20 = (bf16[8,2560]{1,0:T(8,128)(2,1)S(1)}, bf16[8,2560]{1,0:T(8,128)(2,1)S(1)}, u32[]{:S(2)}, u32[]{:S(2)}) collective-permute-start(bf16[8,2560]{1,0:T(8,128)(2,1)S(1)} %maximum_select_fusion.15), channel_id=1, source_target_pairs={{0,4},{4,0},{1,5},{5,1},{2,6},{6,2},{3,7},{7,3},{8,12},{12,8},{9,1... | collective-permute-start | bytes 122888 | tf_op jit(solution)/shard_map/ppermute | solution.py:16
  177.7 23.6 %collective-permute-start.15 = (bf16[8,2560]{1,0:T(8,128)(2,1)S(1)}, bf16[8,2560]{1,0:T(8,128)(2,1)S(1)}, u32[]{:S(2)}, u32[]{:S(2)}) collective-permute-start(bf16[8,2560]{1,0:T(8,128)(2,1)S(1)} %maximum_select_fusion.14), channel_id=1, source_target_pairs={{0,4},{4,0},{1,5},{5,1},{2,6},{6,2},{3,7},{7,3},{8,12},{12,8},{9,1... | collective-permute-start | bytes 122888 | tf_op jit(solution)/shard_map/ppermute | solution.py:16
  186.6 32.3 %collective-permute-start.32 = (bf16[16,2560]{1,0:T(8,128)(2,1)S(1)}, bf16[16,2560]{1,0:T(8,128)(2,1)S(1)}, u32[]{:S(2)}, u32[]{:S(2)}) collective-permute-start(bf16[16,2560]{1,0:T(8,128)(2,1)S(1)} %maximum_select_fusion.12), channel_id=1, source_target_pairs={{0,8},{8,0},{1,9},{9,1},{2,10},{10,2},{3,11},{11,3},{4,12},{12,4},... | collective-permute-start | bytes 245768 | tf_op jit(solution)/shard_map/ppermute | solution.py:16
  195.1 17.4 %collective-permute-start.21 = (bf16[16,2560]{1,0:T(8,128)(2,1)S(1)}, bf16[16,2560]{1,0:T(8,128)(2,1)S(1)}, u32[]{:S(2)}, u32[]{:S(2)}) collective-permute-start(bf16[16,2560]{1,0:T(8,128)(2,1)S(1)} %maximum_select_fusion.11), channel_id=1, source_target_pairs={{0,8},{8,0},{1,9},{9,1},{2,10},{10,2},{3,11},{11,3},{4,12},{12,4},... | collective-permute-start | bytes 245768 | tf_op jit(solution)/shard_map/ppermute | solution.py:16
  201.3 15.0 %collective-permute-start.16 = (bf16[16,2560]{1,0:T(8,128)(2,1)S(1)}, bf16[16,2560]{1,0:T(8,128)(2,1)S(1)}, u32[]{:S(2)}, u32[]{:S(2)}) collective-permute-start(bf16[16,2560]{1,0:T(8,128)(2,1)S(1)} %maximum_select_fusion.10), channel_id=1, source_target_pairs={{0,8},{8,0},{1,9},{9,1},{2,10},{10,2},{3,11},{11,3},{4,12},{12,4},... | collective-permute-start | bytes 245768 | tf_op jit(solution)/shard_map/ppermute | solution.py:16
  246.8 16.0 %collective-permute-start.24 = (f32[16,2560]{1,0:T(8,128)S(1)}, f32[16,2560]{1,0:T(8,128)S(1)}, u32[]{:S(2)}, u32[]{:S(2)}) collective-permute-start(f32[16,2560]{1,0:T(8,128)S(1)} %slice_select_fusion.7), channel_id=1, source_target_pairs={{0,8},{8,0},{1,9},{9,1},{2,10},{10,2},{3,11},{11,3},{4,12},{12,4},... | collective-permute-start | bytes 491528 | tf_op jit(solution)/shard_map/ppermute | solution.py:16
  257.2 17.3 %collective-permute-start.3 = (f32[16,2560]{1,0:T(8,128)S(1)}, f32[16,2560]{1,0:T(8,128)S(1)}, u32[]{:S(2)}, u32[]{:S(2)}) collective-permute-start(f32[16,2560]{1,0:T(8,128)S(1)} %slice_select_fusion.9), channel_id=1, source_target_pairs={{0,8},{8,0},{1,9},{9,1},{2,10},{10,2},{3,11},{11,3},{4,12},{12,4},... | collective-permute-start | bytes 491528 | tf_op jit(solution)/shard_map/ppermute | solution.py:16
  262.9 15.9 %collective-permute-start.25 = (f32[8,2560]{1,0:T(8,128)S(1)}, f32[8,2560]{1,0:T(8,128)S(1)}, u32[]{:S(2)}, u32[]{:S(2)}) collective-permute-start(f32[8,2560]{1,0:T(8,128)S(1)} %slice_select_fusion.11), channel_id=1, source_target_pairs={{0,4},{4,0},{1,5},{5,1},{2,6},{6,2},{3,7},{7,3},{8,12},{12,8},{9,1... | collective-permute-start | bytes 245768 | tf_op jit(solution)/shard_map/ppermute | solution.py:16
  294.5 108.3 %collective-permute-start.6 = (f32[2,2560]{1,0:T(2,128)S(1)}, f32[2,2560]{1,0:T(2,128)S(1)}, u32[]{:S(2)}, u32[]{:S(2)}) collective-permute-start(f32[2,2560]{1,0:T(2,128)S(1)} %broadcast_select_fusion.7), channel_id=1, source_target_pairs={{0,1},{1,0},{2,3},{3,2},{4,5},{5,4},{6,7},{7,6},{8,9},{9,8},{10,11... | collective-permute-start | bytes 61448 | tf_op jit(solution)/shard_map/ppermute | solution.py:16
  406.9 102.9 %collective-permute-start.34 = (bf16[2,2560]{1,0:T(2,128)(2,1)S(1)}, bf16[2,2560]{1,0:T(2,128)(2,1)}, u32[]{:S(2)}, u32[]{:S(2)}) collective-permute-start(bf16[2,2560]{1,0:T(2,128)(2,1)S(1)} %broadcast_select_fusion.2), channel_id=1, source_target_pairs={{0,1},{1,0},{2,3},{3,2},{4,5},{5,4},{6,7},{7,6},{8,9},{9,8},{10,11... | collective-permute-start | bytes 30728 | tf_op jit(solution)/shard_map/ppermute | solution.py:16
  527.6 15.1 %collective-permute-start.37 = (bf16[16,2560]{1,0:T(8,128)(2,1)S(1)}, bf16[16,2560]{1,0:T(8,128)(2,1)S(1)}, u32[]{:S(2)}, u32[]{:S(2)}) collective-permute-start(bf16[16,2560]{1,0:T(8,128)(2,1)S(1)} %maximum_select_fusion.13), channel_id=1, source_target_pairs={{0,8},{8,0},{1,9},{9,1},{2,10},{10,2},{3,11},{11,3},{4,12},{12,4},... | collective-permute-start | bytes 245768 | tf_op jit(solution)/shard_map/ppermute | solution.py:16
  546.8 17.4 %collective-permute-start.8 = (f32[32,2560]{1,0:T(8,128)S(1)}, f32[32,2560]{1,0:T(8,128)S(1)}, u32[]{:S(2)}, u32[]{:S(2)}) collective-permute-start(f32[32,2560]{1,0:T(8,128)S(1)} %slice_select_fusion.4), channel_id=1, source_target_pairs={{0,16},{16,0},{1,17},{17,1},{2,18},{18,2},{3,19},{19,3},{4,20},{20... | collective-permute-start | bytes 983048 | tf_op jit(solution)/shard_map/ppermute | solution.py:16
  555.7 51.0 %collective-permute-start.39 = (f32[32,2560]{1,0:T(8,128)S(1)}, f32[32,2560]{1,0:T(8,128)S(1)}, u32[]{:S(2)}, u32[]{:S(2)}) collective-permute-start(f32[32,2560]{1,0:T(8,128)S(1)} %slice_select_fusion.2), channel_id=1, source_target_pairs={{0,16},{16,0},{1,17},{17,1},{2,18},{18,2},{3,19},{19,3},{4,20},{20... | collective-permute-start | bytes 983048 | tf_op jit(solution)/shard_map/ppermute | solution.py:16
  561.2 478.9 %collective-permute-start.44 = (f32[160,2560]{1,0:T(8,128)}, f32[160,2560]{1,0:T(8,128)}, u32[]{:S(2)}, u32[]{:S(2)}) collective-permute-start(f32[160,2560]{1,0:T(8,128)} %slice_select_fusion.1), channel_id=1, source_target_pairs={{0,32},{32,0},{1,33},{33,1},{2,34},{34,2},{3,35},{35,3},{4,36},{36... | collective-permute-start | bytes 4915208 | tf_op jit(solution)/shard_map/ppermute | solution.py:16
  564.3 18.8 %collective-permute-start.9 = (f32[16,2560]{1,0:T(8,128)S(1)}, f32[16,2560]{1,0:T(8,128)S(1)}, u32[]{:S(2)}, u32[]{:S(2)}) collective-permute-start(f32[16,2560]{1,0:T(8,128)S(1)} %slice_select_fusion.8), channel_id=1, source_target_pairs={{0,8},{8,0},{1,9},{9,1},{2,10},{10,2},{3,11},{11,3},{4,12},{12,4},... | collective-permute-start | bytes 491528 | tf_op jit(solution)/shard_map/ppermute | solution.py:16
  583.1 21.6 %collective-permute-start.10 = (f32[8,2560]{1,0:T(8,128)S(1)}, f32[8,2560]{1,0:T(8,128)S(1)}, u32[]{:S(2)}, u32[]{:S(2)}) collective-permute-start(f32[8,2560]{1,0:T(8,128)S(1)} %slice_select_fusion.12), channel_id=1, source_target_pairs={{0,4},{4,0},{1,5},{5,1},{2,6},{6,2},{3,7},{7,3},{8,12},{12,8},{9,1... | collective-permute-start | bytes 245768 | tf_op jit(solution)/shard_map/ppermute | solution.py:16
  599.2 443.8 %collective-permute-start.45 = (f32[160,2560]{1,0:T(8,128)}, f32[160,2560]{1,0:T(8,128)}, u32[]{:S(2)}, u32[]{:S(2)}) collective-permute-start(f32[160,2560]{1,0:T(8,128)} %slice_select_fusion), channel_id=1, source_target_pairs={{0,32},{32,0},{1,33},{33,1},{2,34},{34,2},{3,35},{35,3},{4,36},{36... | collective-permute-start | bytes 4915208 | tf_op jit(solution)/shard_map/ppermute | solution.py:16
  606.8 19.7 %collective-permute-start.40 = (f32[16,2560]{1,0:T(8,128)S(1)}, f32[16,2560]{1,0:T(8,128)S(1)}, u32[]{:S(2)}, u32[]{:S(2)}) collective-permute-start(f32[16,2560]{1,0:T(8,128)S(1)} %slice_select_fusion.6), channel_id=1, source_target_pairs={{0,8},{8,0},{1,9},{9,1},{2,10},{10,2},{3,11},{11,3},{4,12},{12,4},... | collective-permute-start | bytes 491528 | tf_op jit(solution)/shard_map/ppermute | solution.py:16
  (52 other events, 2194.8 us)
where the time goes:
time: 1050 us
  blocking collectives  713 us (68%)
  starting transfers between devices  202 us (19%)
  waiting for transfers between devices  69.4 us (7%)
  other arithmetic  31.5 us (3%)
  matrix products  15.1 us (1%)
  local copies, waits for them, and re-layouts  13.2 us (1%)
    psum x1, blocking collectives, on_device(): gain_total = gain_total + lax.psum(gain_part, 'peer')  276 us
    all_gather x2, blocking collectives, on_device(): whole_in = lax.all_gather(input_rows, 'peer', axis=0, tiled=True)  230 us
    all_gather x2, blocking collectives, on_device(): gathered = lax.all_gather(d_rounded, 'peer', axis=0, tiled=True)  207 us
    ppermute x44, starting transfers between devices, swapped(): return lax.ppermute(block, axis, route)  197 us
    ppermute x44, waiting for transfers between devices, swapped(): return lax.ppermute(block, axis, route)  69.2 us
  transfers between devices with their start and end apart: 46, of which 20 were waited for; matrix products, arithmetic and copies ran while one was open for 5% of the time, Pallas kernels for 0%

commit v1 on v0

v1 whole, which is shorter than its diff:
```python
import jax
import jax.numpy as jnp
from jax import lax
from jax.experimental import pallas as pl
from jax.experimental.pallas import tpu as pltpu
from jax.sharding import PartitionSpec as P

MESH = pl.DeviceIdType.MESH
EPS = 1e-05
NX, NZ = 4, 16
ROWS = 128
BLOCKS = 20
WIDTH = BLOCKS * 128
LINES = 2 * BLOCKS
UNITS = 160
X0, DY0, ACT0, X1, ACT1, DY1 = range(6)
B0, F0, B1, F1 = range(4)
f32, bf16 = jnp.float32, jnp.bfloat16


def dot(a, b):
    return jnp.dot(a, b, preferred_element_type=f32)


def dot_t(a, b):
    return lax.dot_general(a, b, (((1,), (1,)), ((), ())), preferred_element_type=f32)


def cols(c, n=1):
    return pl.ds(c * 128, n * 128)


def kernel(
    act_ref, first_ref, stored_ref, pend_ref, loss_ref, fw_ref, bw_ref, gain_ref, up_hbm, down_hbm,
    out_ref, grad_ref, upg_hbm, downg_hbm, gaing_ref,
    up, down, gat, nat, xs, dys, normed, dyb, hid, dpre, part, part_in, fsum, wire, wire_in,
    pas, gpart, gx, gz, hot, upg, downg,
    w_sem, zs, zr, xsnd, xrcv, ps, pr, gs, gr, og_sem,
):
    sec = lax.axis_index("section")
    peer = lax.axis_index("peer")
    mx, mz = peer // NZ, lax.rem(peer, NZ)

    def at_z(d):
        return (sec, mx * NZ + lax.rem(mz + d, NZ))

    def at_x(d):
        return (sec, lax.rem(mx + d, NX) * NZ + mz)

    nxt = (lax.rem(sec + 1, 8), peer)
    prv = (lax.rem(sec + 7, 8), peer)

    load_up = pltpu.make_async_copy(up_hbm.at[0], up, w_sem.at[0])
    load_down = pltpu.make_async_copy(down_hbm.at[0], down, w_sem.at[1])
    load_up.start()
    load_down.start()

    barrier = pltpu.get_barrier_semaphore()

    def greet_z(d, _):
        pl.semaphore_signal(barrier, inc=1, device_id=at_z(d), device_id_type=MESH)
        return 0

    lax.fori_loop(1, NZ, greet_z, 0)
    for d in range(1, NX):
        pl.semaphore_signal(barrier, inc=1, device_id=at_x(d), device_id_type=MESH)
    for other in (nxt, prv):
        pl.semaphore_signal(barrier, inc=1, device_id=other, device_id_type=MESH)

    def lines_of(pair):
        flat = pair.astype(f32)
        return jnp.concatenate([flat[:, c * 128 : (c + 1) * 128] for c in range(BLOCKS)], axis=0).astype(bf16)

    gat[X0, 0, 0] = lines_of(stored_ref[0, 0])
    gat[DY0, 0, 0] = lines_of(pend_ref[0])
    gat[ACT0, 0, 0] = lines_of(act_ref[0])
    gat[X1, 0, 0] = lines_of(stored_ref[1, 0])
    pl.semaphore_wait(barrier, NZ - 1 + NX - 1 + 2)

    def z_gather(a):
        def send(n, _):
            step = (n + 1) // 2
            d = jnp.where(lax.rem(n, 2) == 1, NZ // 2 - step, NZ // 2 + step)
            pltpu.make_async_remote_copy(
                src_ref=gat.at[a, 0, 0], dst_ref=gat.at[a, 0, NZ - d], send_sem=zs.at[a], recv_sem=zr.at[a],
                device_id=at_z(d), device_id_type=MESH,
            ).start()
            return 0

        lax.fori_loop(0, NZ - 1, send, 0)

    def wait_bytes(ref, sem):
        pltpu.make_async_copy(ref, ref, sem).wait()

    def x_gather(a):
        wait_bytes(gat.at[a, 0, pl.ds(1, NZ - 1)], zr.at[a])
        for d in range(1, NX):
            pltpu.make_async_remote_copy(
                src_ref=gat.at[a, 0], dst_ref=gat.at[a, NX - d], send_sem=xsnd.at[a], recv_sem=xrcv.at[a],
                device_id=at_x(d), device_id_type=MESH,
            ).start()

    def natural(a, lo, hi):
        def one(q, _):
            nat[pl.ds(q, LINES, stride=64), :] = gat[a, q // NZ, lax.rem(q, NZ)].astype(f32)
            return 0

        lax.fori_loop(lo, hi, one, 0)

    def finish_gather(a):
        natural(a, 0, NZ)
        wait_bytes(gat.at[a, pl.ds(1, NX - 1)], xrcv.at[a])
        natural(a, NZ, NZ * NX)

    def row_of(index):
        i = index // 64
        xr = lax.rem(index, 64) // NZ
        zr_ = lax.rem(index, NZ)
        return 2 * (lax.rem(mx + xr, NX) * NZ + lax.rem(mz + zr_, NZ)) + i

    def one_hot(route):
        down_rows = row_of(lax.broadcasted_iota(jnp.int32, (ROWS, ROWS), 0))
        lane = lax.broadcasted_iota(jnp.int32, (ROWS, ROWS), 1)
        picked = jnp.sum(jnp.where(down_rows == lane, route.astype(f32), 0.0), axis=1, keepdims=True)
        return jnp.where(picked == row_of(lane).astype(f32), 1.0, 0.0)

    def permuted(index, dst):
        turn = hot[index]
        for c in range(0, BLOCKS, 2):
            both = jnp.concatenate([nat[pl.ds(c * 128, 128), :], nat[pl.ds(c * 128 + 128, 128), :]], axis=1)
            got = dot(turn, both.astype(bf16))
            dst[pl.ds(c * 128, 128), :] = got[:, :128]
            dst[pl.ds(c * 128 + 128, 128), :] = got[:, 128:]

    def norm(into):
        total = jnp.zeros((ROWS, 128), f32)
        for c in range(BLOCKS):
            block = xs[pl.ds(c * 128, 128), :]
            total = total + block * block
        inv = lax.rsqrt(jnp.sum(total, axis=1, keepdims=True) * (1.0 / WIDTH) + EPS)
        for c in range(BLOCKS):
            block = xs[pl.ds(c * 128, 128), :]
            into[:, c * 128 : (c + 1) * 128] = (block * inv * gain_ref[:, c * 128 : (c + 1) * 128]).astype(bf16)
        return inv

    def put_part(r, c, block):
        low = block.astype(bf16)
        for xr in range(NX):
            for i in range(2):
                part[r, xr, c, pl.ds(i * 16, 16), :] = low[i * 64 + xr * 16 : i * 64 + xr * 16 + 16, :]

    def x_sum(r):
        for d in range(1, NX):
            pltpu.make_async_remote_copy(
                src_ref=part.at[r, d], dst_ref=part_in.at[r, NX - 1 - d], send_sem=xsnd.at[6 + r], recv_sem=xrcv.at[6 + r],
                device_id=at_x(d), device_id_type=MESH,
            ).start()

    def z_sum(r):
        wait_bytes(part_in.at[r], xrcv.at[6 + r])

        def add(c, _):
            total = part[r, 0, c].astype(f32)
            for k in range(NX - 1):
                total = total + part_in[r, k, c].astype(f32)
            fsum[r, pl.ds(pl.multiple_of(c * 32, 32), 32), :] = total
            return 0

        lax.fori_loop(0, BLOCKS, add, 0)

        def send(n, _):
            step = (n + 1) // 2
            d = jnp.where(lax.rem(n, 2) == 1, NZ // 2 - step, NZ // 2 + step)
            wire[r, d] = fsum[r, pl.ds(d, LINES, stride=16), :].astype(bf16)
            pltpu.make_async_remote_copy(
                src_ref=wire.at[r, d], dst_ref=wire_in.at[r, NZ - d], send_sem=zs.at[6 + r], recv_sem=zr.at[6 + r],
                device_id=at_z(d), device_id_type=MESH,
            ).start()
            return 0

        lax.fori_loop(0, NZ - 1, send, 0)

    def finish_sum(r):
        wait_bytes(wire_in.at[r, pl.ds(1, NZ - 1)], zr.at[6 + r])
        total = fsum[r, pl.ds(0, LINES, stride=16), :]
        for k in range(1, NZ):
            total = total + wire_in[r, k].astype(f32)
        return total

    def own_lines(ref):
        return ref[pl.ds(0, LINES, stride=64), :]

    def forward(r, tick):
        permuted(tick, xs)
        norm(normed.at[2])
        pre = dot_t(normed[2], up[...])
        hidden = (pre / (1.0 + jnp.exp(-pre))).astype(bf16)
        for c in range(0, BLOCKS, 2):
            branch = dot(hidden, down[:, c * 128 : (c + 2) * 128])
            put_part(r, c, branch[:, :128])
            put_part(r, c + 1, branch[:, 128:])
        x_sum(r)
        return own_lines(xs)

    def backward_inputs(tick, a_x):
        permuted(2 + tick, xs)
        inv = norm(normed.at[tick])
        pre = dot_t(normed[tick], up[...])
        return inv, pre

    def backward(r, tick, inv, pre):
        permuted(2 + tick, dys)
        for c in range(BLOCKS):
            dyb[tick, :, c * 128 : (c + 1) * 128] = dys[pl.ds(c * 128, 128), :].astype(bf16)
        d_hidden = dot_t(dyb[tick], down[...])
        sig = 1.0 / (1.0 + jnp.exp(-pre))
        hid[:, tick * ROWS : (tick + 1) * ROWS] = (pre * sig).T.astype(bf16)
        d_pre = d_hidden * sig * (1.0 + pre * (1.0 - sig))
        dpre[:, tick * ROWS : (tick + 1) * ROWS] = d_pre.T.astype(bf16)
        d_pre = d_pre.astype(bf16)
        for c in range(0, BLOCKS, 2):
            d_norm = dot(d_pre, up[:, c * 128 : (c + 2) * 128])
            for k in range(2):
                block = d_norm[:, k * 128 : (k + 1) * 128]
                put_part(r, c + k, block)
                line = jnp.sum(block * (xs[pl.ds((c + k) * 128, 128), :] * inv), axis=0, keepdims=True)
                if tick == 0:
                    gpart[c + k : c + k + 1, :] = line
                else:
                    gpart[c + k : c + k + 1, :] += line
        x_sum(r)
        return own_lines(xs), own_lines(dys)

    even = lax.rem(lax.broadcasted_iota(jnp.int32, (LINES, 128), 0), 2) == 0

    def row_means(v):
        first = jnp.sum(jnp.where(even, v, 0.0), keepdims=True)
        second = jnp.sum(jnp.where(even, 0.0, v), keepdims=True)
        return jnp.where(even, first, second) * (1.0 / WIDTH)

    gain_lines = jnp.concatenate(
        [jnp.broadcast_to(gain_ref[:, c * 128 : (c + 1) * 128], (2, 128)) for c in range(BLOCKS)], axis=0
    )

    def input_grad(d_norm, x, dy):
        inv = lax.rsqrt(row_means(x * x) + EPS)
        scaled = d_norm * gain_lines
        return dy + inv * scaled - x * (inv * inv * inv) * row_means(scaled * x)

    def put_pair(ref, tick, value):
        for c in range(BLOCKS):
            ref[tick, 0, :, c * 128 : (c + 1) * 128] = value[2 * c : 2 * c + 2, :].astype(bf16)

    def hand_on(k, value, other, a):
        pas[k] = value
        pltpu.make_async_remote_copy(
            src_ref=pas.at[k], dst_ref=gat.at[a, 0, 0], send_sem=ps.at[k], recv_sem=pr.at[k],
            device_id=other, device_id_type=MESH,
        ).start()

    z_gather(X0)
    z_gather(DY0)
    z_gather(ACT0)
    for tick in range(2):
        hot[tick] = one_hot(fw_ref[tick, pl.ds(sec, 1), :]).astype(bf16)
        hot[2 + tick] = one_hot(bw_ref[tick, pl.ds(sec, 1), :]).T.astype(bf16)
    x_gather(X0)
    x_gather(DY0)
    x_gather(ACT0)
    z_gather(X1)
    load_up.wait()
    load_down.wait()
    finish_gather(X0)
    inv, pre = backward_inputs(0, X0)
    finish_gather(DY0)
    x_own, dy_own = backward(B0, 0, inv, pre)
    finish_gather(ACT0)
    act_own = forward(F0, 0)
    z_sum(B0)
    z_sum(F0)
    x_gather(X1)
    grad = input_grad(finish_sum(B0), x_own, dy_own).astype(bf16)
    hand_on(1, jnp.where(sec == 0, lines_of(loss_ref[0]), grad), prv, DY1)
    out = (act_own + finish_sum(F0)).astype(bf16)
    hand_on(0, jnp.where(sec == 7, lines_of(first_ref[0]), out), nxt, ACT1)
    put_pair(grad_ref, 0, grad.astype(f32))
    put_pair(out_ref, 0, out.astype(f32))

    wait_bytes(gat.at[DY1, 0, 0], pr.at[1])
    z_gather(DY1)
    wait_bytes(gat.at[ACT1, 0, 0], pr.at[0])
    z_gather(ACT1)
    finish_gather(X1)
    inv, pre = backward_inputs(1, X1)
    x_gather(DY1)
    x_gather(ACT1)
    finish_gather(DY1)
    x_own, dy_own = backward(B1, 1, inv, pre)

    for d in range(1, NX):
        pltpu.make_async_remote_copy(
            src_ref=gpart, dst_ref=gx.at[NX - d], send_sem=gs.at[0], recv_sem=gr.at[0],
            device_id=at_x(d), device_id_type=MESH,
        ).start()
    gx[0] = gpart[...]

    finish_gather(ACT1)
    act_own = forward(F1, 1)
    wait_bytes(gx.at[pl.ds(1, NX - 1)], gr.at[0])
    total = jnp.zeros((BLOCKS, 128), f32)
    for k in range(NX):
        total = total + gx[lax.rem(k - mx + NX, NX)]
    gz[0] = total

    def gain_send(d, _):
        pltpu.make_async_remote_copy(
            src_ref=gz.at[0], dst_ref=gz.at[NZ - d], send_sem=gs.at[1], recv_sem=gr.at[1],
            device_id=at_z(d), device_id_type=MESH,
        ).start()
        return 0

    z_sum(B1)
    lax.fori_loop(1, NZ, gain_send, 0)
    z_sum(F1)

    for c in range(0, BLOCKS, 4):
        part_cols = slice(c * 128, (c + 4) * 128)
        both = jnp.concatenate([normed[0, :, part_cols], normed[1, :, part_cols]], axis=0)
        upg[:, part_cols] = (dot(dpre[...], both) * 0.5).astype(bf16)
        both = jnp.concatenate([dyb[0, :, part_cols], dyb[1, :, part_cols]], axis=0)
        downg[:, part_cols] = (dot(hid[...], both) * 0.5).astype(bf16)
    store_up = pltpu.make_async_copy(upg, upg_hbm.at[0], og_sem.at[0])
    store_down = pltpu.make_async_copy(downg, downg_hbm.at[0], og_sem.at[1])
    store_up.start()
    store_down.start()

    put_pair(grad_ref, 1, input_grad(finish_sum(B1), x_own, dy_own))
    put_pair(out_ref, 1, act_own + finish_sum(F1))
    wait_bytes(gz.at[pl.ds(1, NZ - 1)], gr.at[1])
    total = jnp.zeros((BLOCKS, 128), f32)
    for k in range(NZ):
        total = total + gz[lax.rem(k - mz + NZ, NZ)]
    for c in range(BLOCKS):
        gaing_ref[:, c * 128 : (c + 1) * 128] = total[c : c + 1, :]

    for a in range(6):
        wait_bytes(gat.at[a, 0, pl.ds(1, NZ - 1)], zs.at[a])
        wait_bytes(gat.at[a, pl.ds(1, NX - 1)], xsnd.at[a])
    for r in range(4):
        wait_bytes(part.at[r, pl.ds(1, NX - 1)], xsnd.at[6 + r])
        wait_bytes(wire.at[r, pl.ds(1, NZ - 1)], zs.at[6 + r])
    for k in range(2):
        wait_bytes(pas.at[k], ps.at[k])
    wait_bytes(gx.at[pl.ds(1, NX - 1)], gs.at[0])
    wait_bytes(gz.at[pl.ds(1, NZ - 1)], gs.at[1])
    store_up.wait()
    store_down.wait()


def on_device(*args):
    vmem = pl.BlockSpec(memory_space=pltpu.VMEM)
    anywhere = pl.BlockSpec(memory_space=pl.ANY)
    return pl.pallas_call(
        kernel,
        out_shape=(
            jax.ShapeDtypeStruct((2, 1, 2, WIDTH), bf16),
            jax.ShapeDtypeStruct((2, 1, 2, WIDTH), bf16),
            jax.ShapeDtypeStruct((1, UNITS, WIDTH), bf16),
            jax.ShapeDtypeStruct((1, UNITS, WIDTH), bf16),
            jax.ShapeDtypeStruct((1, WIDTH), f32),
        ),
        in_specs=[vmem] * 8 + [anywhere] * 2,
        out_specs=(vmem, vmem, anywhere, anywhere, vmem),
        scratch_shapes=[
            pltpu.VMEM((UNITS, WIDTH), bf16),
            pltpu.VMEM((UNITS, WIDTH), bf16),
            pltpu.VMEM((6, NX, NZ, LINES, 128), bf16),
            pltpu.VMEM((BLOCKS * ROWS, 128), f32),
            pltpu.VMEM((BLOCKS * ROWS, 128), f32),
            pltpu.VMEM((BLOCKS * ROWS, 128), f32),
            pltpu.VMEM((3, ROWS, WIDTH), bf16),
            pltpu.VMEM((2, ROWS, WIDTH), bf16),
            pltpu.VMEM((UNITS, 2 * ROWS), bf16),
            pltpu.VMEM((UNITS, 2 * ROWS), bf16),
            pltpu.VMEM((4, NX, BLOCKS, 32, 128), bf16),
            pltpu.VMEM((4, NX - 1, BLOCKS, 32, 128), bf16),
            pltpu.VMEM((4, BLOCKS * 32, 128), f32),
            pltpu.VMEM((4, NZ, LINES, 128), bf16),
            pltpu.VMEM((4, NZ, LINES, 128), bf16),
            pltpu.VMEM((2, LINES, 128), bf16),
            pltpu.VMEM((BLOCKS, 128), f32),
            pltpu.VMEM((NX, BLOCKS, 128), f32),
            pltpu.VMEM((NZ, BLOCKS, 128), f32),
            pltpu.VMEM((4, ROWS, ROWS), bf16),
            pltpu.VMEM((UNITS, WIDTH), bf16),
            pltpu.VMEM((UNITS, WIDTH), bf16),
            pltpu.SemaphoreType.DMA((2,)),
            pltpu.SemaphoreType.DMA((10,)),
            pltpu.SemaphoreType.DMA((10,)),
            pltpu.SemaphoreType.DMA((10,)),
            pltpu.SemaphoreType.DMA((10,)),
            pltpu.SemaphoreType.DMA((2,)),
            pltpu.SemaphoreType.DMA((2,)),
            pltpu.SemaphoreType.DMA((2,)),
            pltpu.SemaphoreType.DMA((2,)),
            pltpu.SemaphoreType.DMA((2,)),
        ],
        compiler_params=pltpu.CompilerParams(
            collective_id=0, has_side_effects=True, vmem_limit_bytes=56 * 1024 * 1024
        ),
    )(*args)


def solution(mesh):
    placed = (
        P("section", "peer", None),
        P(None, "peer", None),
        P(None, "section", "peer", None),
        P("section", "peer", None),
        P(None, "peer", None),
        P(),
        P(),
        P("section", None),
        P("section", "peer", None),
        P("section", "peer", None),
    )
    return jax.shard_map(
        on_device,
        mesh=mesh,
        in_specs=placed,
        out_specs=(
            P(None, "section", "peer", None),
            P(None, "section", "peer", None),
            P("section", "peer", None),
            P("section", "peer", None),
            P("section", None),
        ),
        check_vma=False,
    )
```

time: 1050 us -> 139 us (0.13)
  the two profiles are of different devices: /device:TPU:16 before, /device:TPU:8 now
where the time goes in v1:
time: 139 us
  Pallas kernels  132 us (95%)
  local copies, waits for them, and re-layouts  5.62 us (4%)
    pallas_call x1, Pallas kernels, on_device(): pl.pallas_call(kernel, out_shape=(jax.ShapeDtypeStruct((2, 1, 2, WIDTH),...  132 us
    unnamed x11, local copies, waits for them, and re-layouts  5.62 us

profile of v1, /device:TPU:8, one launch (start us, length us, event | category | flops | bytes accessed | tf_op | source)
XLA Modules:
  0.0 138.5 jit_solution(16143056355193200110)
XLA Ops:
  0.6 132.2 %shard_map.137 = (bf16[2,1,2,2560]{3,2,1,0:T(2,128)(2,1)}, bf16[2,1,2,2560]{3,2,1,0:T(2,128)(2,1)}, bf16[1,160,2560]{2,1,0:T(8,128)(2,1)}, bf16[1,160,2560]{2,1,0:T(8,128)(2,1)}, f32[1,2560]{1,0:T(1,128)}) custom-call(bf16[1,2,2560]{2,1,0:T(2,128)(2,1)} %act_ref.1, bf16[1,2,2560]{2,1,0:T(2,128)(2,1)} %first_ref.1, bf16[2,1,2,2560]{3,2,1,0:T(2,128)(2,1)} %stored_ref.1, ...), custom_call_target="tpu_custom_call" | custom-call | tf_op jit(solution)/shard_map/pallas_call | solution.py:363
  132.9 0.0 copy-start.1
  132.9 1.4 copy.20
  134.3 0.0 copy-done.1
  134.3 0.6 copy.21
  134.9 0.0 copy-start
  134.9 2.2 %copy.22 = bf16[1,160,2560]{2,1,0:T(8,128)(2,1)} copy(bf16[1,160,2560]{2,1,0:T(8,128)(2,1)} %get-tuple-element.12) | data formatting | bytes 1638400
  137.0 0.0 copy-done
  137.0 0.0 copy-start.2
  137.0 0.9 copy.23
  137.9 0.0 copy-done.2
  137.9 0.6 copy.24
Async XLA Ops:
  132.9 1.4 copy-start.1
  134.9 2.2 %copy-start = (bf16[1,160,2560]{2,1,0:T(8,128)(2,1)S(1)}, bf16[1,160,2560]{2,1,0:T(8,128)(2,1)}, u32[]{:S(2)}) copy-start(bf16[1,160,2560]{2,1,0:T(8,128)(2,1)} %get-tuple-element.13) | copy-start | bytes 2457604
  137.0 0.9 copy-start.2

commit v2 on v0

v2 whole, which is shorter than its diff:
```python
import jax
import jax.numpy as jnp
from jax import lax
from jax.experimental import pallas as pl
from jax.experimental.pallas import tpu as pltpu
from jax.sharding import PartitionSpec as P

MESH = pl.DeviceIdType.MESH
EPS = 1e-05
NX, NZ = 4, 16
ROWS = 128
BLOCKS = 5
SLICE = BLOCKS * 128
WIDTH = NX * SLICE
LINES = 8 * BLOCKS
PAIR = 2 * BLOCKS
UNITS = 160
X0, DY0, ACT0, X1, ACT1, DY1 = range(6)
B0, F0, B1, F1 = range(4)
PRE_B0, DH_B0, PRE_F0, PRE_B1, DH_B1, PRE_F1 = range(6)
IN_B0, IN_F0, IN_B1, IN_F1 = range(4)
f32, bf16 = jnp.float32, jnp.bfloat16


def dot(a, b):
    return jnp.dot(a, b, preferred_element_type=f32)


def dot_t(a, b):
    return lax.dot_general(a, b, (((1,), (1,)), ((), ())), preferred_element_type=f32)


def t_dot(a, b):
    return lax.dot_general(a, b, (((0,), (0,)), ((), ())), preferred_element_type=f32)


def wait_bytes(ref, sem):
    pltpu.make_async_copy(ref, ref, sem).wait()


def kernel(
    act_ref, first_ref, stored_ref, pend_ref, loss_ref, fw_ref, bw_ref, gain_ref, up_hbm, down_hbm,
    out_ref, grad_ref, upg_hbm, downg_hbm, gaing_ref,
    wu, wd, msgf, msg_out, msg_in, lines, gat, nat, xs, xg, dyb, fs, wire, rin, fin,
    xown, xo, xi, sq, ag, mm, full, hid, dpre, gpart, gz, gx, pas, resf, ro, ri, hot, upg, downg,
    w_sem, ws, wr, ms, mr, zs, zr, zs2, zr2, xsn, xrc, sqs, sqr, ags, agr, mms, mmr, fus, fur, ps, pr, rs, rr,
    gs, gr, og_sem,
):
    sec = lax.axis_index("section")
    peer = lax.axis_index("peer")
    mx, mz = peer // NZ, lax.rem(peer, NZ)
    even = lax.rem(mz, 2) == 0

    def at_z(d):
        return (sec, mx * NZ + lax.rem(mz + (d + NZ), NZ))

    def at_x(d):
        return (sec, lax.rem(mx + d, NX) * NZ + mz)

    nxt = (lax.rem(sec + 1, 8), peer)
    prv = (lax.rem(sec + 7, 8), peer)

    def send(src, dst, ssem, rsem, dev):
        pltpu.make_async_remote_copy(
            src_ref=src, dst_ref=dst, send_sem=ssem, recv_sem=rsem, device_id=dev, device_id_type=MESH
        ).start()

    def slice_of(x):
        return pl.ds(pl.multiple_of(x * SLICE, 128), SLICE)

    def rel(x):
        return lax.rem(x - mx + NX, NX)

    barrier = pltpu.get_barrier_semaphore()
    greeted = [at_z(d) for d in (1, 2, 3, 4, -1, -2, -3, -4)] + [at_x(d) for d in (1, 2, 3)] + [nxt, prv]
    for other in greeted:
        pl.semaphore_signal(barrier, inc=1, device_id=other, device_id_type=MESH)

    own_up = pltpu.make_async_copy(up_hbm.at[0, :, slice_of(mx)], wu.at[0], w_sem.at[0])
    own_down = pltpu.make_async_copy(down_hbm.at[0, :, slice_of(mx)], wd.at[0], w_sem.at[1])
    own_up.start()
    own_down.start()

    pairs = [stored_ref[0, 0], pend_ref[0], act_ref[0], stored_ref[1, 0], first_ref[0], loss_ref[0]]
    for x in range(NX):
        msgf[x, pl.ds(56, 8), :] = jnp.zeros((8, 128), f32)
    for a, pair in enumerate(pairs):
        flat = pair.astype(f32)
        for x in range(NX):
            for c in range(BLOCKS):
                col = (x * BLOCKS + c) * 128
                msgf[x, pl.ds(a * PAIR + 2 * c, 2), :] = flat[:, col : col + 128]
    for x in range(NX):
        msg_out[x] = msgf[x].astype(bf16)
    pl.semaphore_wait(barrier, len(greeted))

    for d in (2, 1, 3):
        send(msg_out.at[lax.rem(mx + d, NX)], msg_in.at[NX - d], ms.at[0], mr.at[0], at_x(d))
    for k, (src, dst) in enumerate(((up_hbm, wu), (down_hbm, wd))):
        for d in (2, 1, 3):
            send(src.at[0, :, slice_of(lax.rem(mx + d, NX))], dst.at[NX - d], ws.at[k], wr.at[k], at_x(d))
    msg_in[0] = msg_out[mx]
    wait_bytes(msg_in.at[pl.ds(1, NX - 1)], mr.at[0])
    for x in range(NX):
        got = msg_in[rel(x)].astype(f32)
        for a in range(6):
            for c in range(BLOCKS):
                lines[a, pl.ds(8 * c + 2 * x, 2), :] = got[a * PAIR + 2 * c : a * PAIR + 2 * c + 2, :]

    def z_first(buf, ssem, rsem):
        send(buf.at[0], buf.at[12], ssem, rsem.at[0], at_z(4))
        send(buf.at[0], buf.at[4], ssem, rsem.at[1], at_z(-4))
        for d in (3, 2, 1):
            send(buf.at[0], buf.at[NZ - d], ssem, rsem.at[2], at_z(d))
            send(buf.at[0], buf.at[d], ssem, rsem.at[3], at_z(-d))

    def z_relay(buf, ssem, rsem):
        wait_bytes(buf.at[12], rsem.at[0])
        wait_bytes(buf.at[4], rsem.at[1])
        send(buf.at[jnp.where(even, 12, 4)], buf.at[8], ssem, rsem.at[4], at_z(jnp.where(even, 4, -4)))
        for d in (3, 2, 1):
            send(buf.at[12], buf.at[12 - d], ssem, rsem.at[5], at_z(d))
            send(buf.at[4], buf.at[4 + d], ssem, rsem.at[6], at_z(-d))

    def z_done(buf, rsem):
        wait_bytes(buf.at[pl.ds(13, 3)], rsem.at[2])
        wait_bytes(buf.at[pl.ds(1, 3)], rsem.at[3])
        wait_bytes(buf.at[8], rsem.at[4])
        wait_bytes(buf.at[pl.ds(9, 3)], rsem.at[5])
        wait_bytes(buf.at[pl.ds(5, 3)], rsem.at[6])

    def gather_first(a):
        z_first(gat.at[a], zs.at[a], zr.at[a])

    def gather_relay(a):
        z_relay(gat.at[a], zs.at[a], zr.at[a])

    for a in (X0, DY0, ACT0, X1):
        gat[a, 0] = lines[a].astype(bf16)
    gather_first(X0)
    gather_first(DY0)
    gather_first(ACT0)

    def sum_first(r):
        def fill(k):
            wire[r, k] = fs[r, pl.ds(k, LINES, stride=NZ), :].astype(bf16)

        for k in (8, 7, 9, 6, 10, 5, 11):
            fill(k)
        send(wire.at[r, 8], rin.at[r, 6], zs2.at[r], zr2.at[r, 0], at_z(jnp.where(even, 4, -4)))
        for d in (3, 2, 1):
            send(wire.at[r, 4 + d], rin.at[r, d - 1], zs2.at[r], zr2.at[r, 0], at_z(d))
            send(wire.at[r, 12 - d], rin.at[r, 2 + d], zs2.at[r], zr2.at[r, 0], at_z(-d))
        for d in (3, 2, 1):
            fill(d)
            fill(NZ - d)
            send(wire.at[r, d], fin.at[r, d - 1], zs2.at[r], zr2.at[r, 1], at_z(d))
            send(wire.at[r, NZ - d], fin.at[r, 2 + d], zs2.at[r], zr2.at[r, 1], at_z(-d))

    def sum_relay(r):
        ahead = fs[r, pl.ds(4, LINES, stride=NZ), :]
        behind = fs[r, pl.ds(12, LINES, stride=NZ), :]
        wait_bytes(rin.at[r], zr2.at[r, 0])
        across = rin[r, 6].astype(f32)
        for k in range(3):
            ahead = ahead + rin[r, k].astype(f32)
            behind = behind + rin[r, 3 + k].astype(f32)
        wire[r, 4] = (ahead + jnp.where(even, across, 0.0)).astype(bf16)
        wire[r, 12] = (behind + jnp.where(even, 0.0, across)).astype(bf16)
        send(wire.at[r, 4], fin.at[r, 6], zs2.at[r], zr2.at[r, 1], at_z(4))
        send(wire.at[r, 12], fin.at[r, 7], zs2.at[r], zr2.at[r, 1], at_z(-4))

    def sum_done(r):
        total = fs[r, pl.ds(0, LINES, stride=NZ), :]
        wait_bytes(fin.at[r], zr2.at[r, 1])
        for k in range(8):
            total = total + fin[r, k].astype(f32)
        return total

    def row_of(index):
        group = index // NZ
        return 2 * ((group // 2) * NZ + lax.rem(mz + lax.rem(index, NZ), NZ)) + lax.rem(group, 2)

    lane = lax.broadcasted_iota(jnp.int32, (ROWS, ROWS), 1)
    placed = row_of(lax.broadcasted_iota(jnp.int32, (ROWS, ROWS), 0)) == lane
    lane_row = row_of(lane).astype(f32)

    def one_hot(route):
        picked = jnp.sum(jnp.where(placed, route.astype(f32), 0.0), axis=1, keepdims=True)
        return jnp.where(picked == lane_row, 1.0, 0.0)

    for tick in range(2):
        hot[tick] = one_hot(fw_ref[tick, pl.ds(sec, 1), :]).astype(bf16)
        hot[2 + tick] = one_hot(bw_ref[tick, pl.ds(sec, 1), :]).T.astype(bf16)

    gain = gain_ref[:, slice_of(mx)]
    gain_of = [gain[:, c * 128 : (c + 1) * 128] for c in range(BLOCKS)]

    def block(c):
        return slice(c * 128, (c + 1) * 128)

    def turned(a, index):
        z_done(gat.at[a], zr.at[a])
        for k in range(NZ):
            nat[pl.ds(k, LINES, stride=NZ), :] = gat[a, k].astype(f32)
        both = jnp.concatenate([nat[pl.ds(c * 128, 128), :] for c in range(BLOCKS)], axis=1)
        return dot(hot[index], both.astype(bf16))

    def take_input(a, e, index):
        got = turned(a, index)
        total = jnp.zeros((ROWS, 128), f32)
        for c in range(BLOCKS):
            part = got[:, block(c)]
            xs[e, pl.ds(c * 128, 128), :] = part
            xg[e, :, block(c)] = (part * gain_of[c]).astype(bf16)
            total = total + part * part
        sq[e, 0] = jnp.broadcast_to(jnp.sum(total.T, axis=0, keepdims=True), (8, 128))
        for d in (2, 1, 3):
            send(sq.at[e, 0], sq.at[e, NX - d], sqs.at[e], sqr.at[e], at_x(d))

    def take_grad(a, tick, index):
        got = turned(a, index)
        dyb[tick] = got.astype(bf16)
        own = [got[0:1, :]]
        for c in range(BLOCKS):
            lines[tick, pl.ds(8 * c, 8), :] = jnp.concatenate(
                [got[16 * k : 16 * k + 1, block(c)] for k in range(8)], axis=0
            )

    def x_parts(e, weight, rows):
        for d in (2, 1, 3):
            xo[e, d] = dot_t(weight[d], rows).astype(bf16)
            send(xo.at[e, d], xi.at[e, NX - d], xsn.at[e], xrc.at[e], at_x(d))
        xown[e] = dot_t(weight[0], rows)

    def x_total(e):
        wait_bytes(xi.at[e, pl.ds(1, NX - 1)], xrc.at[e])
        total = xown[e]
        for k in range(1, NX):
            total = total + xi[e, k].astype(f32)
        return total

    def x_gather(g, value):
        ag[g, 0] = value
        for d in (2, 1, 3):
            send(ag.at[g, 0], ag.at[g, NX - d], ags.at[g], agr.at[g], at_x(d))

    def x_gathered(g):
        wait_bytes(ag.at[g, pl.ds(1, NX - 1)], agr.at[g])
        return ag[g].reshape(NX * UNITS, ROWS)

    def inv_rms(e):
        wait_bytes(sq.at[e, pl.ds(1, NX - 1)], sqr.at[e])
        total = sq[e, 0] + sq[e, 1] + sq[e, 2] + sq[e, 3]
        return lax.rsqrt(total[0:1, :] * (1.0 / WIDTH) + EPS)

    def by_row(value):
        return jnp.broadcast_to(value, (ROWS, ROWS)).T

    def spread_full(n, value):
        for c in range(BLOCKS):
            full[n, 0, :, block(c)] = value(c)
        for d in (2, 1, 3):
            send(full.at[n, 0], full.at[n, NX - d], fus.at[n], fur.at[n], at_x(d))

    def normed_block(e, inv_rows):
        return lambda c: (xs[e, pl.ds(c * 128, 128), :] * inv_rows * gain_of[c]).astype(bf16)

    def own_lines(ref):
        return ref[pl.ds(0, LINES, stride=NZ), :]

    def hidden_forward(e, pre_e, g):
        pre = x_total(pre_e) * inv_rms(e)
        x_gather(g, (pre / (1.0 + jnp.exp(-pre))).astype(bf16))

    def branch_forward(r, g):
        branch = t_dot(x_gathered(g), wd[...].reshape(NX * UNITS, SLICE))
        for c in range(BLOCKS):
            fs[r, pl.ds(c * 128, 128), :] = branch[:, block(c)]
        sum_first(r)

    def pre_backward(e, pre_e, tick):
        inv = inv_rms(e)
        pre = x_total(pre_e) * inv
        sig = 1.0 / (1.0 + jnp.exp(-pre))
        hid[:, tick * ROWS : (tick + 1) * ROWS] = (pre * sig).astype(bf16)
        return inv, pre, sig * (1.0 + pre * (1.0 - sig))

    def d_pre_backward(tick, dh_e, g, pre, slope):
        d_pre = (x_total(dh_e) * slope).astype(bf16)
        x_gather(g, d_pre)
        dpre[:, tick * ROWS : (tick + 1) * ROWS] = d_pre
        mm[tick, 0] = jnp.broadcast_to(jnp.sum(d_pre.astype(f32) * pre, axis=0, keepdims=True), (8, 128))
        for d in (2, 1, 3):
            send(mm.at[tick, 0], mm.at[tick, NX - d], mms.at[tick], mmr.at[tick], at_x(d))

    def branch_backward(r, g, e, tick, inv, inv_rows):
        d_norm = t_dot(x_gathered(g), wu[...].reshape(NX * UNITS, SLICE))
        wait_bytes(mm.at[tick, pl.ds(1, NX - 1)], mmr.at[tick])
        total = (mm[tick, 0] + mm[tick, 1] + mm[tick, 2] + mm[tick, 3])[0:1, :]
        back = by_row(total * inv * inv * (1.0 / WIDTH))
        for c in range(BLOCKS):
            x = xs[e, pl.ds(c * 128, 128), :]
            part = d_norm[:, block(c)] * inv_rows
            fs[r, pl.ds(c * 128, 128), :] = part * gain_of[c] - x * back
            line = jnp.sum(part * x, axis=0, keepdims=True)
            if tick == 0:
                gpart[c : c + 1, :] = line
            else:
                gpart[c : c + 1, :] += line
        sum_first(r)

    def hand_on(k, value, other, a):
        pas[k] = value
        send(pas.at[k], gat.at[a, 0], ps.at[k], pr.at[k], other)

    def results_out(q, value):
        resf[q] = value
        for x in range(NX):
            ro[q, x] = jnp.concatenate(
                [resf[q, pl.ds(8 * c + 2 * x, 2), :] for c in range(BLOCKS)] + [jnp.zeros((6, 128), f32)], axis=0
            ).astype(bf16)
        for d in (2, 1, 3):
            send(ro.at[q, lax.rem(mx + d, NX)], ri.at[q, NX - d], rs.at[q], rr.at[q], at_x(d))
        ri[q, 0] = ro[q, mx]

    def results_in(q, ref, tick):
        wait_bytes(ri.at[q, pl.ds(1, NX - 1)], rr.at[q])
        for x in range(NX):
            got = ri[q, rel(x)].astype(f32)
            for c in range(BLOCKS):
                col = (x * BLOCKS + c) * 128
                ref[tick, 0, :, col : col + 128] = got[2 * c : 2 * c + 2, :].astype(bf16)

    first_lines = lines[4].astype(bf16)
    loss_lines = lines[5].astype(bf16)
    gather_relay(X0)
    gather_relay(DY0)
    gather_relay(ACT0)
    gather_first(X1)
    take_input(X0, IN_B0, 2)
    own_up.wait()
    wait_bytes(wu.at[pl.ds(1, NX - 1)], wr.at[0])
    x_parts(PRE_B0, wu, xg[IN_B0])
    take_grad(DY0, 0, 2)
    own_down.wait()
    wait_bytes(wd.at[pl.ds(1, NX - 1)], wr.at[1])
    x_parts(DH_B0, wd, dyb[0])
    take_input(ACT0, IN_F0, 0)
    x_parts(PRE_F0, wu, xg[IN_F0])
    gather_relay(X1)
    inv, pre, slope = pre_backward(IN_B0, PRE_B0, 0)
    d_pre_backward(0, DH_B0, 0, pre, slope)
    hidden_forward(IN_F0, PRE_F0, 1)
    inv_rows = by_row(inv)
    branch_backward(B0, 0, IN_B0, 0, inv, inv_rows)
    branch_forward(F0, 1)
    spread_full(0, normed_block(IN_B0, inv_rows))
    sum_relay(B0)
    sum_relay(F0)
    spread_full(1, lambda c: dyb[0, :, block(c)])
    grad = (sum_done(B0) + lines[0]).astype(bf16)
    hand_on(1, jnp.where(sec == 0, loss_lines, grad), prv, DY1)
    out = (sum_done(F0) + own_lines(xs.at[IN_F0])).astype(bf16)
    hand_on(0, jnp.where(sec == 7, first_lines, out), nxt, ACT1)
    take_input(X1, IN_B1, 3)
    x_parts(PRE_B1, wu, xg[IN_B1])

    wait_bytes(gat.at[DY1, 0], pr.at[1])
    gather_first(DY1)
    wait_bytes(gat.at[ACT1, 0], pr.at[0])
    gather_first(ACT1)
    results_out(0, out.astype(f32))
    results_out(1, grad.astype(f32))
    inv, pre, slope = pre_backward(IN_B1, PRE_B1, 1)
    inv_rows = by_row(inv)
    gather_relay(DY1)
    gather_relay(ACT1)
    spread_full(2, normed_block(IN_B1, inv_rows))
    take_grad(DY1, 1, 3)
    x_parts(DH_B1, wd, dyb[1])
    take_input(ACT1, IN_F1, 1)
    x_parts(PRE_F1, wu, xg[IN_F1])
    d_pre_backward(1, DH_B1, 2, pre, slope)
    hidden_forward(IN_F1, PRE_F1, 3)
    spread_full(3, lambda c: dyb[1, :, block(c)])
    branch_backward(B1, 2, IN_B1, 1, inv, inv_rows)
    branch_forward(F1, 3)
    gz[0] = jnp.concatenate([gpart[...], jnp.zeros((8 - BLOCKS, 128), f32)], axis=0)
    z_first(gz, gs.at[0], gr)
    sum_relay(B1)
    sum_relay(F1)
    z_relay(gz, gs.at[0], gr)
    results_in(0, out_ref, 0)
    results_in(1, grad_ref, 0)

    for n in range(4):
        wait_bytes(full.at[n, pl.ds(1, NX - 1)], fur.at[n])
    stores = []
    for x in range(NX):
        where = slice_of(lax.rem(mx + x, NX))
        for k, (left, at, grads, hbm) in enumerate(((dpre, 0, upg, upg_hbm), (hid, 1, downg, downg_hbm))):
            both = jnp.concatenate([full[at, x], full[2 + at, x]], axis=0)
            grads[x] = (dot(left[...], both) * 0.5).astype(bf16)
            store = pltpu.make_async_copy(grads.at[x], hbm.at[0, :, where], og_sem.at[k, x])
            store.start()
            stores.append(store)

    results_out(2, sum_done(B1) + lines[1])
    results_out(3, sum_done(F1) + own_lines(xs.at[IN_F1]))
    z_done(gz, gr)
    total = jnp.zeros((8, 128), f32)
    for z in range(NZ):
        total = total + gz[lax.rem(z - mz + NZ, NZ)]
    gx[0] = total
    for d in (2, 1, 3):
        send(gx.at[0], gx.at[NX - d], gs.at[1], gr.at[7], at_x(d))
    results_in(2, grad_ref, 1)
    results_in(3, out_ref, 1)
    wait_bytes(gx.at[pl.ds(1, NX - 1)], gr.at[7])
    for x in range(NX):
        got = gx[rel(x)]
        for c in range(BLOCKS):
            col = (x * BLOCKS + c) * 128
            gaing_ref[:, col : col + 128] = got[c : c + 1, :]

    three = pl.ds(1, NX - 1)
    wait_bytes(msg_in.at[three], ms.at[0])
    wait_bytes(wu.at[three], ws.at[0])
    wait_bytes(wd.at[three], ws.at[1])
    for a in range(6):
        wait_bytes(gat.at[a, pl.ds(1, NZ - 1)], zs.at[a])
        wait_bytes(xi.at[a, three], xsn.at[a])
    for r in range(4):
        wait_bytes(wire.at[r, pl.ds(1, NZ - 1)], zs2.at[r])
        wait_bytes(sq.at[r, three], sqs.at[r])
        wait_bytes(ag.at[r, three], ags.at[r])
        wait_bytes(full.at[r, three], fus.at[r])
        wait_bytes(ri.at[r, three], rs.at[r])
    for k in range(2):
        wait_bytes(mm.at[k, three], mms.at[k])
        wait_bytes(pas.at[k], ps.at[k])
    wait_bytes(gz.at[pl.ds(1, NZ - 1)], gs.at[0])
    wait_bytes(gx.at[three], gs.at[1])
    for store in stores:
        store.wait()


def on_device(*args):
    vmem = pl.BlockSpec(memory_space=pltpu.VMEM)
    anywhere = pl.BlockSpec(memory_space=pl.ANY)
    dma = pltpu.SemaphoreType.DMA
    shapes = (
        jax.ShapeDtypeStruct((2, 1, 2, WIDTH), bf16),
        jax.ShapeDtypeStruct((2, 1, 2, WIDTH), bf16),
        jax.ShapeDtypeStruct((1, UNITS, WIDTH), bf16),
        jax.ShapeDtypeStruct((1, UNITS, WIDTH), bf16),
        jax.ShapeDtypeStruct((1, WIDTH), f32),
    )
    return pl.pallas_call(
        kernel,
        out_shape=shapes,
        in_specs=[vmem] * 8 + [anywhere] * 2,
        out_specs=(vmem, vmem, anywhere, anywhere, vmem),
        scratch_shapes=[
            pltpu.VMEM((NX, UNITS, SLICE), bf16),
            pltpu.VMEM((NX, UNITS, SLICE), bf16),
            pltpu.VMEM((NX, 64, 128), f32),
            pltpu.VMEM((NX, 64, 128), bf16),
            pltpu.VMEM((NX, 64, 128), bf16),
            pltpu.VMEM((6, LINES, 128), f32),
            pltpu.VMEM((6, NZ, LINES, 128), bf16),
            pltpu.VMEM((SLICE, 128), f32),
            pltpu.VMEM((4, SLICE, 128), f32),
            pltpu.VMEM((4, ROWS, SLICE), bf16),
            pltpu.VMEM((2, ROWS, SLICE), bf16),
            pltpu.VMEM((4, SLICE, 128), f32),
            pltpu.VMEM((4, NZ, LINES, 128), bf16),
            pltpu.VMEM((4, 7, LINES, 128), bf16),
            pltpu.VMEM((4, 8, LINES, 128), bf16),
            pltpu.VMEM((6, UNITS, ROWS), f32),
            pltpu.VMEM((6, NX, UNITS, ROWS), bf16),
            pltpu.VMEM((6, NX, UNITS, ROWS), bf16),
            pltpu.VMEM((4, NX, 8, 128), f32),
            pltpu.VMEM((4, NX, UNITS, ROWS), bf16),
            pltpu.VMEM((2, NX, 8, 128), f32),
            pltpu.VMEM((4, NX, ROWS, SLICE), bf16),
            pltpu.VMEM((UNITS, 2 * ROWS), bf16),
            pltpu.VMEM((UNITS, 2 * ROWS), bf16),
            pltpu.VMEM((BLOCKS, 128), f32),
            pltpu.VMEM((NZ, 8, 128), f32),
            pltpu.VMEM((NX, 8, 128), f32),
            pltpu.VMEM((2, LINES, 128), bf16),
            pltpu.VMEM((4, LINES, 128), f32),
            pltpu.VMEM((4, NX, 16, 128), bf16),
            pltpu.VMEM((4, NX, 16, 128), bf16),
            pltpu.VMEM((4, ROWS, ROWS), bf16),
            pltpu.VMEM((NX, UNITS, SLICE), bf16),
            pltpu.VMEM((NX, UNITS, SLICE), bf16),
            dma((2,)),
            dma((2,)),
            dma((2,)),
            dma((1,)),
            dma((1,)),
            dma((6,)),
            dma((6, 7)),
            dma((4,)),
            dma((4, 2)),
            dma((6,)),
            dma((6,)),
            dma((4,)),
            dma((4,)),
            dma((4,)),
            dma((4,)),
            dma((2,)),
            dma((2,)),
            dma((4,)),
            dma((4,)),
            dma((2,)),
            dma((2,)),
            dma((4,)),
            dma((4,)),
            dma((2,)),
            dma((8,)),
            dma((2, NX)),
        ],
        compiler_params=pltpu.CompilerParams(
            collective_id=0, has_side_effects=True, vmem_limit_bytes=56 * 1024 * 1024
        ),
    )(*args)


def solution(mesh):
    placed = (
        P("section", "peer", None),
        P(None, "peer", None),
        P(None, "section", "peer", None),
        P("section", "peer", None),
        P(None, "peer", None),
        P(),
        P(),
        P("section", None),
        P("section", "peer", None),
        P("section", "peer", None),
    )
    return jax.shard_map(
        on_device,
        mesh=mesh,
        in_specs=placed,
        out_specs=(
            P(None, "section", "peer", None),
            P(None, "section", "peer", None),
            P("section", "peer", None),
            P("section", "peer", None),
            P("section", None),
        ),
        check_vma=False,
    )
```

time: 1050 us -> 107 us (0.10)
  the two profiles are of different devices: /device:TPU:16 before, /device:TPU:8 now
where the time goes in v2:
time: 107 us
  Pallas kernels  101 us (94%)
  local copies, waits for them, and re-layouts  5.62 us (5%)
    pallas_call x1, Pallas kernels, on_device(): pl.pallas_call(kernel, out_shape=shapes, in_specs=[vmem] * 8 + [anywhere]...  101 us
    unnamed x11, local copies, waits for them, and re-layouts  5.62 us

profile of v2, /device:TPU:8, one launch (start us, length us, event | category | flops | bytes accessed | tf_op | source)
XLA Modules:
  0.0 107.0 jit_solution(1486271399217240657)
XLA Ops:
  0.6 100.7 %shard_map.137 = (bf16[2,1,2,2560]{3,2,1,0:T(2,128)(2,1)}, bf16[2,1,2,2560]{3,2,1,0:T(2,128)(2,1)}, bf16[1,160,2560]{2,1,0:T(8,128)(2,1)}, bf16[1,160,2560]{2,1,0:T(8,128)(2,1)}, f32[1,2560]{1,0:T(1,128)}) custom-call(bf16[1,2,2560]{2,1,0:T(2,128)(2,1)} %act_ref.1, bf16[1,2,2560]{2,1,0:T(2,128)(2,1)} %first_ref.1, bf16[2,1,2,2560]{3,2,1,0:T(2,128)(2,1)} %stored_ref.1, ...), custom_call_target="tpu_custom_call" | custom-call | tf_op jit(solution)/shard_map/pallas_call | solution.py:460
  101.3 0.0 copy-start.1
  101.3 1.4 %copy.20 = bf16[2,1,2,2560]{3,2,1,0:T(2,128)(2,1)} copy(bf16[2,1,2,2560]{3,2,1,0:T(2,128)(2,1)} %get-tuple-element.10) | data formatting | bytes 40960
  102.7 0.0 copy-done.1
  102.7 0.6 copy.21
  103.3 0.0 copy-start
  103.3 2.2 %copy.22 = bf16[1,160,2560]{2,1,0:T(8,128)(2,1)} copy(bf16[1,160,2560]{2,1,0:T(8,128)(2,1)} %get-tuple-element.12) | data formatting | bytes 1638400
  105.5 0.0 copy-done
  105.5 0.0 copy-start.2
  105.5 0.9 copy.23
  106.4 0.0 copy-done.2
  106.4 0.6 copy.24
Async XLA Ops:
  101.3 1.4 %copy-start.1 = (bf16[2,1,2,2560]{3,2,1,0:T(2,128)(2,1)S(1)}, bf16[2,1,2,2560]{3,2,1,0:T(2,128)(2,1)}, u32[]{:S(2)}) copy-start(bf16[2,1,2,2560]{3,2,1,0:T(2,128)(2,1)} %get-tuple-element.11) | copy-start | bytes 61444
  103.3 2.2 %copy-start = (bf16[1,160,2560]{2,1,0:T(8,128)(2,1)S(1)}, bf16[1,160,2560]{2,1,0:T(8,128)(2,1)}, u32[]{:S(2)}) copy-start(bf16[1,160,2560]{2,1,0:T(8,128)(2,1)} %get-tuple-element.13) | copy-start | bytes 2457604
  105.5 0.9 copy-start.2

commit v3 on v2

--- a/solution.py
+++ b/solution.py
@@ -44,21 +44,20 @@
     wu, wd, msgf, msg_out, msg_in, lines, gat, nat, xs, xg, dyb, fs, wire, rin, fin,
     xown, xo, xi, sq, ag, mm, full, hid, dpre, gpart, gz, gx, pas, resf, ro, ri, hot, upg, downg,
     w_sem, ws, wr, ms, mr, zs, zr, zs2, zr2, xsn, xrc, sqs, sqr, ags, agr, mms, mmr, fus, fur, ps, pr, rs, rr,
-    gs, gr, og_sem,
+    gs, gr, og_sem, ready,
 ):
     sec = lax.axis_index("section")
     peer = lax.axis_index("peer")
     mx, mz = peer // NZ, lax.rem(peer, NZ)
     even = lax.rem(mz, 2) == 0
 
-    def at_z(d):
-        return (sec, mx * NZ + lax.rem(mz + (d + NZ), NZ))
+    after, before = lax.rem(sec + 1, 8), lax.rem(sec + 7, 8)
+
+    def at_z(d, section=sec):
+        return (section, mx * NZ + lax.rem(mz + (d + NZ), NZ))
 
     def at_x(d):
         return (sec, lax.rem(mx + d, NX) * NZ + mz)
-
-    nxt = (lax.rem(sec + 1, 8), peer)
-    prv = (lax.rem(sec + 7, 8), peer)
 
     def send(src, dst, ssem, rsem, dev):
         pltpu.make_async_remote_copy(
@@ -72,7 +71,8 @@
         return lax.rem(x - mx + NX, NX)
 
     barrier = pltpu.get_barrier_semaphore()
-    greeted = [at_z(d) for d in (1, 2, 3, 4, -1, -2, -3, -4)] + [at_x(d) for d in (1, 2, 3)] + [nxt, prv]
+    steps = (1, 2, 3, 4, -1, -2, -3, -4)
+    greeted = [at_z(d) for d in steps] + [at_x(d) for d in (1, 2, 3)] + [at_z(0, after), at_z(0, before)]
     for other in greeted:
         pl.semaphore_signal(barrier, inc=1, device_id=other, device_id_type=MESH)
 
@@ -93,6 +93,8 @@
     for x in range(NX):
         msg_out[x] = msgf[x].astype(bf16)
     pl.semaphore_wait(barrier, len(greeted))
+    pl.semaphore_signal(ready.at[0], inc=1, device_id=at_z(0, before), device_id_type=MESH)
+    pl.semaphore_signal(ready.at[1], inc=1, device_id=at_z(0, after), device_id_type=MESH)
 
     for d in (2, 1, 3):
         send(msg_out.at[lax.rem(mx + d, NX)], msg_in.at[NX - d], ms.at[0], mr.at[0], at_x(d))
@@ -107,12 +109,12 @@
             for c in range(BLOCKS):
                 lines[a, pl.ds(8 * c + 2 * x, 2), :] = got[a * PAIR + 2 * c : a * PAIR + 2 * c + 2, :]
 
-    def z_first(buf, ssem, rsem):
-        send(buf.at[0], buf.at[12], ssem, rsem.at[0], at_z(4))
-        send(buf.at[0], buf.at[4], ssem, rsem.at[1], at_z(-4))
+    def z_first(src, buf, ssem, rsem, section=sec):
+        send(src, buf.at[12], ssem, rsem.at[0], at_z(4, section))
+        send(src, buf.at[4], ssem, rsem.at[1], at_z(-4, section))
         for d in (3, 2, 1):
-            send(buf.at[0], buf.at[NZ - d], ssem, rsem.at[2], at_z(d))
-            send(buf.at[0], buf.at[d], ssem, rsem.at[3], at_z(-d))
+            send(src, buf.at[NZ - d], ssem, rsem.at[2], at_z(d, section))
+            send(src, buf.at[d], ssem, rsem.at[3], at_z(-d, section))
 
     def z_relay(buf, ssem, rsem):
         wait_bytes(buf.at[12], rsem.at[0])
@@ -122,24 +124,26 @@
             send(buf.at[12], buf.at[12 - d], ssem, rsem.at[5], at_z(d))
             send(buf.at[4], buf.at[4 + d], ssem, rsem.at[6], at_z(-d))
 
-    def z_done(buf, rsem):
+    def z_near(buf, rsem):
         wait_bytes(buf.at[pl.ds(13, 3)], rsem.at[2])
         wait_bytes(buf.at[pl.ds(1, 3)], rsem.at[3])
+
+    def z_far(buf, rsem):
         wait_bytes(buf.at[8], rsem.at[4])
         wait_bytes(buf.at[pl.ds(9, 3)], rsem.at[5])
         wait_bytes(buf.at[pl.ds(5, 3)], rsem.at[6])
 
     def gather_first(a):
-        z_first(gat.at[a], zs.at[a], zr.at[a])
+        z_first(gat.at[a, 0], gat.at[a], zs.at[a], zr.at[a])
 
     def gather_relay(a):
         z_relay(gat.at[a], zs.at[a], zr.at[a])
 
     for a in (X0, DY0, ACT0, X1):
         gat[a, 0] = lines[a].astype(bf16)
+    gather_first(ACT0)
     gather_first(X0)
     gather_first(DY0)
-    gather_first(ACT0)
 
     def sum_first(r):
         def fill(k):
@@ -200,8 +204,11 @@
         return slice(c * 128, (c + 1) * 128)
 
     def turned(a, index):
-        z_done(gat.at[a], zr.at[a])
-        for k in range(NZ):
+        z_near(gat.at[a], zr.at[a])
+        for k in (0, 1, 2, 3, 4, 12, 13, 14, 15):
+            nat[pl.ds(k, LINES, stride=NZ), :] = gat[a, k].astype(f32)
+        z_far(gat.at[a], zr.at[a])
+        for k in range(5, 12):
             nat[pl.ds(k, LINES, stride=NZ), :] = gat[a, k].astype(f32)
         both = jnp.concatenate([nat[pl.ds(c * 128, 128), :] for c in range(BLOCKS)], axis=1)
         return dot(hot[index], both.astype(bf16))
@@ -221,17 +228,17 @@
     def take_grad(a, tick, index):
         got = turned(a, index)
         dyb[tick] = got.astype(bf16)
-        own = [got[0:1, :]]
         for c in range(BLOCKS):
             lines[tick, pl.ds(8 * c, 8), :] = jnp.concatenate(
                 [got[16 * k : 16 * k + 1, block(c)] for k in range(8)], axis=0
             )
 
     def x_parts(e, weight, rows):
-        for d in (2, 1, 3):
-            xo[e, d] = dot_t(weight[d], rows).astype(bf16)
+        parts = dot_t(weight[...].reshape(NX * UNITS, SLICE), rows)
+        for d in (2, 1, 3):
+            xo[e, d] = parts[d * UNITS : (d + 1) * UNITS, :].astype(bf16)
             send(xo.at[e, d], xi.at[e, NX - d], xsn.at[e], xrc.at[e], at_x(d))
-        xown[e] = dot_t(weight[0], rows)
+        xown[e] = parts[:UNITS, :]
 
     def x_total(e):
         wait_bytes(xi.at[e, pl.ds(1, NX - 1)], xrc.at[e])
@@ -310,9 +317,11 @@
                 gpart[c : c + 1, :] += line
         sum_first(r)
 
-    def hand_on(k, value, other, a):
+    def hand_on(k, value, section, a):
         pas[k] = value
-        send(pas.at[k], gat.at[a, 0], ps.at[k], pr.at[k], other)
+        pl.semaphore_wait(ready.at[k], 1)
+        z_first(pas.at[k], gat.at[a], zs.at[a], zr.at[a], section)
+        send(pas.at[k], gat.at[a, 0], ps.at[k], pr.at[k], at_z(0, section))
 
     def results_out(q, value):
         resf[q] = value
@@ -332,89 +341,90 @@
                 col = (x * BLOCKS + c) * 128
                 ref[tick, 0, :, col : col + 128] = got[2 * c : 2 * c + 2, :].astype(bf16)
 
+    stores = []
+
+    def weight_grad(left, n, grads, hbm):
+        wait_bytes(full.at[n, pl.ds(1, NX - 1)], fur.at[n])
+        wait_bytes(full.at[2 + n, pl.ds(1, NX - 1)], fur.at[2 + n])
+        for x in range(NX):
+            both = jnp.concatenate([full[n, x], full[2 + n, x]], axis=0)
+            grads[x] = (dot(left[...], both) * 0.5).astype(bf16)
+            where = slice_of(lax.rem(mx + x, NX))
+            stores.append(pltpu.make_async_copy(grads.at[x], hbm.at[0, :, where], og_sem.at[n, x]))
+            stores[-1].start()
+
     first_lines = lines[4].astype(bf16)
     loss_lines = lines[5].astype(bf16)
+    gather_relay(ACT0)
     gather_relay(X0)
     gather_relay(DY0)
-    gather_relay(ACT0)
     gather_first(X1)
-    take_input(X0, IN_B0, 2)
+    take_input(ACT0, IN_F0, 0)
     own_up.wait()
     wait_bytes(wu.at[pl.ds(1, NX - 1)], wr.at[0])
+    x_parts(PRE_F0, wu, xg[IN_F0])
+    take_input(X0, IN_B0, 2)
     x_parts(PRE_B0, wu, xg[IN_B0])
     take_grad(DY0, 0, 2)
     own_down.wait()
     wait_bytes(wd.at[pl.ds(1, NX - 1)], wr.at[1])
     x_parts(DH_B0, wd, dyb[0])
-    take_input(ACT0, IN_F0, 0)
-    x_parts(PRE_F0, wu, xg[IN_F0])
-    gather_relay(X1)
+    hidden_forward(IN_F0, PRE_F0, 1)
     inv, pre, slope = pre_backward(IN_B0, PRE_B0, 0)
     d_pre_backward(0, DH_B0, 0, pre, slope)
-    hidden_forward(IN_F0, PRE_F0, 1)
+    gather_relay(X1)
     inv_rows = by_row(inv)
+    spread_full(0, normed_block(IN_B0, inv_rows))
+    branch_forward(F0, 1)
     branch_backward(B0, 0, IN_B0, 0, inv, inv_rows)
-    branch_forward(F0, 1)
-    spread_full(0, normed_block(IN_B0, inv_rows))
-    sum_relay(B0)
-    sum_relay(F0)
-    spread_full(1, lambda c: dyb[0, :, block(c)])
-    grad = (sum_done(B0) + lines[0]).astype(bf16)
-    hand_on(1, jnp.where(sec == 0, loss_lines, grad), prv, DY1)
-    out = (sum_done(F0) + own_lines(xs.at[IN_F0])).astype(bf16)
-    hand_on(0, jnp.where(sec == 7, first_lines, out), nxt, ACT1)
     take_input(X1, IN_B1, 3)
     x_parts(PRE_B1, wu, xg[IN_B1])
-
-    wait_bytes(gat.at[DY1, 0], pr.at[1])
-    gather_first(DY1)
-    wait_bytes(gat.at[ACT1, 0], pr.at[0])
-    gather_first(ACT1)
+    sum_relay(F0)
+    sum_relay(B0)
+    spread_full(1, lambda c: dyb[0, :, block(c)])
+    out = (sum_done(F0) + own_lines(xs.at[IN_F0])).astype(bf16)
+    hand_on(0, jnp.where(sec == 7, first_lines, out), after, ACT1)
+    grad = (sum_done(B0) + lines[0]).astype(bf16)
+    hand_on(1, jnp.where(sec == 0, loss_lines, grad), before, DY1)
+
     results_out(0, out.astype(f32))
     results_out(1, grad.astype(f32))
     inv, pre, slope = pre_backward(IN_B1, PRE_B1, 1)
     inv_rows = by_row(inv)
+    spread_full(2, normed_block(IN_B1, inv_rows))
+    gather_relay(ACT1)
     gather_relay(DY1)
-    gather_relay(ACT1)
-    spread_full(2, normed_block(IN_B1, inv_rows))
+    wait_bytes(gat.at[ACT1, 0], pr.at[0])
+    take_input(ACT1, IN_F1, 1)
+    x_parts(PRE_F1, wu, xg[IN_F1])
+    wait_bytes(gat.at[DY1, 0], pr.at[1])
     take_grad(DY1, 1, 3)
     x_parts(DH_B1, wd, dyb[1])
-    take_input(ACT1, IN_F1, 1)
-    x_parts(PRE_F1, wu, xg[IN_F1])
+    hidden_forward(IN_F1, PRE_F1, 3)
     d_pre_backward(1, DH_B1, 2, pre, slope)
-    hidden_forward(IN_F1, PRE_F1, 3)
     spread_full(3, lambda c: dyb[1, :, block(c)])
+    branch_forward(F1, 3)
     branch_backward(B1, 2, IN_B1, 1, inv, inv_rows)
-    branch_forward(F1, 3)
     gz[0] = jnp.concatenate([gpart[...], jnp.zeros((8 - BLOCKS, 128), f32)], axis=0)
-    z_first(gz, gs.at[0], gr)
+    z_first(gz.at[0], gz, gs.at[0], gr)
+    sum_relay(F1)
     sum_relay(B1)
-    sum_relay(F1)
     z_relay(gz, gs.at[0], gr)
+    weight_grad(dpre, 0, upg, upg_hbm)
     results_in(0, out_ref, 0)
     results_in(1, grad_ref, 0)
-
-    for n in range(4):
-        wait_bytes(full.at[n, pl.ds(1, NX - 1)], fur.at[n])
-    stores = []
-    for x in range(NX):
-        where = slice_of(lax.rem(mx + x, NX))
-        for k, (left, at, grads, hbm) in enumerate(((dpre, 0, upg, upg_hbm), (hid, 1, downg, downg_hbm))):
-            both = jnp.concatenate([full[at, x], full[2 + at, x]], axis=0)
-            grads[x] = (dot(left[...], both) * 0.5).astype(bf16)
-            store = pltpu.make_async_copy(grads.at[x], hbm.at[0, :, where], og_sem.at[k, x])
-            store.start()
-            stores.append(store)
-
+    results_out(3, sum_done(F1) + own_lines(xs.at[IN_F1]))
     results_out(2, sum_done(B1) + lines[1])
-    results_out(3, sum_done(F1) + own_lines(xs.at[IN_F1]))
-    z_done(gz, gr)
+    z_near(gz, gr)
+    z_far(gz, gr)
     total = jnp.zeros((8, 128), f32)
     for z in range(NZ):
         total = total + gz[lax.rem(z - mz + NZ, NZ)]
     gx[0] = total
     for d in (2, 1, 3):
         send(gx.at[0], gx.at[NX - d], gs.at[1], gr.at[7], at_x(d))
+
+    weight_grad(hid, 1, downg, downg_hbm)
     results_in(2, grad_ref, 1)
     results_in(3, out_ref, 1)
     wait_bytes(gx.at[pl.ds(1, NX - 1)], gr.at[7])
@@ -446,6 +456,20 @@
         store.wait()
 
 
+def place(*refs):
+    sources, targets, held, sem = refs[:5], refs[5:10], refs[10:15], refs[15]
+    loads, stores = [], []
+    for k in range(5):
+        loads.append(pltpu.make_async_copy(sources[k], held[k], sem.at[0, k]))
+        loads[k].start()
+    for k in range(5):
+        loads[k].wait()
+        stores.append(pltpu.make_async_copy(held[k], targets[k], sem.at[1, k]))
+        stores[k].start()
+    for store in stores:
+        store.wait()
+
+
 def on_device(*args):
     vmem = pl.BlockSpec(memory_space=pltpu.VMEM)
     anywhere = pl.BlockSpec(memory_space=pl.ANY)
@@ -457,7 +481,7 @@
         jax.ShapeDtypeStruct((1, UNITS, WIDTH), bf16),
         jax.ShapeDtypeStruct((1, WIDTH), f32),
     )
-    return pl.pallas_call(
+    results = pl.pallas_call(
         kernel,
         out_shape=shapes,
         in_specs=[vmem] * 8 + [anywhere] * 2,
@@ -523,11 +547,19 @@
             dma((2,)),
             dma((8,)),
             dma((2, NX)),
+            pltpu.SemaphoreType.REGULAR((2,)),
         ],
         compiler_params=pltpu.CompilerParams(
             collective_id=0, has_side_effects=True, vmem_limit_bytes=56 * 1024 * 1024
         ),
     )(*args)
+    return pl.pallas_call(
+        place,
+        out_shape=shapes,
+        in_specs=[anywhere] * 5,
+        out_specs=(anywhere,) * 5,
+        scratch_shapes=[pltpu.VMEM(shape.shape, shape.dtype) for shape in shapes] + [dma((2, 5))],
+    )(*results)
 
 
 def solution(mesh):

time: 107 us -> 98.3 us (0.919)
  the two profiles are of different devices: /device:TPU:8 before, /device:TPU:16 now
where the time goes in v3:
time: 98.3 us; the launch traced here: 98.1 us
  Pallas kernels  97.5 us (99%)
    pallas_call x1, Pallas kernels, on_device(): pl.pallas_call(kernel, out_shape=shapes, in_specs=[vmem] * 8 + [anywhere]...  95.1 us
    pallas_call x1, Pallas kernels, on_device(): pl.pallas_call(place, out_shape=shapes, in_specs=[anywhere] * 5, out_spec...  2.43 us

profile of v3, /device:TPU:16, one launch (start us, length us, event | category | flops | bytes accessed | tf_op | source)
XLA Modules:
  0.0 98.1 jit_solution(10378720826397274408)
XLA Ops:
  0.6 95.1 %shard_map.137 = (bf16[2,1,2,2560]{3,2,1,0:T(2,128)(2,1)}, bf16[2,1,2,2560]{3,2,1,0:T(2,128)(2,1)}, bf16[1,160,2560]{2,1,0:T(8,128)(2,1)}, bf16[1,160,2560]{2,1,0:T(8,128)(2,1)}, f32[1,2560]{1,0:T(1,128)}) custom-call(bf16[1,2,2560]{2,1,0:T(2,128)(2,1)} %act_ref.1, bf16[1,2,2560]{2,1,0:T(2,128)(2,1)} %first_ref.1, bf16[2,1,2,2560]{3,2,1,0:T(2,128)(2,1)} %stored_ref.1, ...), custom_call_target="tpu_custom_call" | custom-call | tf_op jit(solution)/shard_map/pallas_call | solution.py:484
  95.7 2.4 %shard_map.138 = (bf16[2,1,2,2560]{3,2,1,0:T(2,128)(2,1)}, bf16[2,1,2,2560]{3,2,1,0:T(2,128)(2,1)}, bf16[1,160,2560]{2,1,0:T(8,128)(2,1)}, bf16[1,160,2560]{2,1,0:T(8,128)(2,1)}, f32[1,2560]{1,0:T(1,128)}) custom-call(bf16[2,1,2,2560]{3,2,1,0:T(2,128)(2,1)} %get-tuple-element.10.refs_0_, bf16[2,1,2,2560]{3,2,1,0:T(2,128)(2,1)} %get-tuple-element.11.refs_1_, ...), custom_call_target="tpu_custom_call" | custom-call | tf_op jit(solution)/shard_map/pallas_call | solution.py:556

commit v4 on v3

--- a/solution.py
+++ b/solution.py
@@ -39,9 +39,9 @@
 
 
 def kernel(
-    act_ref, first_ref, stored_ref, pend_ref, loss_ref, fw_ref, bw_ref, gain_ref, up_hbm, down_hbm,
+    act_hbm, first_hbm, stored_hbm, pend_hbm, loss_hbm, fw_hbm, bw_hbm, gain_hbm, up_hbm, down_hbm,
     out_ref, grad_ref, upg_hbm, downg_hbm, gaing_ref,
-    wu, wd, msgf, msg_out, msg_in, lines, gat, nat, xs, xg, dyb, fs, wire, rin, fin,
+    act_ref, first_ref, stored_ref, pend_ref, loss_ref, fw_ref, bw_ref, gain_ref, wu, wd, msgf, msg_out, msg_in, lines, gat, nat, xs, xg, dyb, fs, wire, rin, fin,
     xown, xo, xi, sq, ag, mm, full, hid, dpre, gpart, gz, gx, pas, resf, ro, ri, hot, upg, downg,
     w_sem, ws, wr, ms, mr, zs, zr, zs2, zr2, xsn, xrc, sqs, sqr, ags, agr, mms, mmr, fus, fur, ps, pr, rs, rr,
     gs, gr, og_sem, ready,
@@ -76,10 +76,25 @@
     for other in greeted:
         pl.semaphore_signal(barrier, inc=1, device_id=other, device_id_type=MESH)
 
+    loads = [
+        pltpu.make_async_copy(source, target, w_sem.at[2 + n])
+        for n, (source, target) in enumerate(
+            (
+                (stored_hbm, stored_ref), (pend_hbm, pend_ref), (act_hbm, act_ref), (first_hbm, first_ref),
+                (loss_hbm, loss_ref), (fw_hbm, fw_ref), (bw_hbm, bw_ref), (gain_hbm, gain_ref),
+            )
+        )
+    ]
+    for load in loads:
+        load.start()
+
     own_up = pltpu.make_async_copy(up_hbm.at[0, :, slice_of(mx)], wu.at[0], w_sem.at[0])
     own_down = pltpu.make_async_copy(down_hbm.at[0, :, slice_of(mx)], wd.at[0], w_sem.at[1])
     own_up.start()
     own_down.start()
+
+    for load in loads:
+        load.wait()
 
     pairs = [stored_ref[0, 0], pend_ref[0], act_ref[0], stored_ref[1, 0], first_ref[0], loss_ref[0]]
     for x in range(NX):
@@ -103,11 +118,13 @@
             send(src.at[0, :, slice_of(lax.rem(mx + d, NX))], dst.at[NX - d], ws.at[k], wr.at[k], at_x(d))
     msg_in[0] = msg_out[mx]
     wait_bytes(msg_in.at[pl.ds(1, NX - 1)], mr.at[0])
-    for x in range(NX):
-        got = msg_in[rel(x)].astype(f32)
-        for a in range(6):
-            for c in range(BLOCKS):
-                lines[a, pl.ds(8 * c + 2 * x, 2), :] = got[a * PAIR + 2 * c : a * PAIR + 2 * c + 2, :]
+
+    def take_lines(arrays):
+        for x in range(NX):
+            got = msg_in[rel(x)].astype(f32)
+            for a in arrays:
+                for c in range(BLOCKS):
+                    lines[a, pl.ds(8 * c + 2 * x, 2), :] = got[a * PAIR + 2 * c : a * PAIR + 2 * c + 2, :]
 
     def z_first(src, buf, ssem, rsem, section=sec):
         send(src, buf.at[12], ssem, rsem.at[0], at_z(4, section))
@@ -139,26 +156,30 @@
     def gather_relay(a):
         z_relay(gat.at[a], zs.at[a], zr.at[a])
 
-    for a in (X0, DY0, ACT0, X1):
+    take_lines((X0, DY0))
+    for a in (X0, DY0):
         gat[a, 0] = lines[a].astype(bf16)
+        gather_first(a)
+    take_lines((ACT0, X1, 4, 5))
+    gat[ACT0, 0] = lines[ACT0].astype(bf16)
     gather_first(ACT0)
-    gather_first(X0)
-    gather_first(DY0)
+    gat[X1, 0] = lines[X1].astype(bf16)
 
     def sum_first(r):
         def fill(k):
             wire[r, k] = fs[r, pl.ds(k, LINES, stride=NZ), :].astype(bf16)
 
-        for k in (8, 7, 9, 6, 10, 5, 11):
-            fill(k)
+        fill(8)
         send(wire.at[r, 8], rin.at[r, 6], zs2.at[r], zr2.at[r, 0], at_z(jnp.where(even, 4, -4)))
         for d in (3, 2, 1):
+            fill(4 + d)
             send(wire.at[r, 4 + d], rin.at[r, d - 1], zs2.at[r], zr2.at[r, 0], at_z(d))
+            fill(12 - d)
             send(wire.at[r, 12 - d], rin.at[r, 2 + d], zs2.at[r], zr2.at[r, 0], at_z(-d))
         for d in (3, 2, 1):
             fill(d)
+            send(wire.at[r, d], fin.at[r, d - 1], zs2.at[r], zr2.at[r, 1], at_z(d))
             fill(NZ - d)
-            send(wire.at[r, d], fin.at[r, d - 1], zs2.at[r], zr2.at[r, 1], at_z(d))
             send(wire.at[r, NZ - d], fin.at[r, 2 + d], zs2.at[r], zr2.at[r, 1], at_z(-d))
 
     def sum_relay(r):
@@ -315,6 +336,9 @@
                 gpart[c : c + 1, :] = line
             else:
                 gpart[c : c + 1, :] += line
+        if tick == 1:
+            gz[0] = jnp.concatenate([gpart[...], jnp.zeros((8 - BLOCKS, 128), f32)], axis=0)
+            z_first(gz.at[0], gz, gs.at[0], gr)
         sum_first(r)
 
     def hand_on(k, value, section, a):
@@ -355,65 +379,62 @@
 
     first_lines = lines[4].astype(bf16)
     loss_lines = lines[5].astype(bf16)
-    gather_relay(ACT0)
     gather_relay(X0)
     gather_relay(DY0)
-    gather_first(X1)
-    take_input(ACT0, IN_F0, 0)
+    gather_relay(ACT0)
+    take_input(X0, IN_B0, 2)
     own_up.wait()
     wait_bytes(wu.at[pl.ds(1, NX - 1)], wr.at[0])
-    x_parts(PRE_F0, wu, xg[IN_F0])
-    take_input(X0, IN_B0, 2)
     x_parts(PRE_B0, wu, xg[IN_B0])
     take_grad(DY0, 0, 2)
     own_down.wait()
     wait_bytes(wd.at[pl.ds(1, NX - 1)], wr.at[1])
     x_parts(DH_B0, wd, dyb[0])
-    hidden_forward(IN_F0, PRE_F0, 1)
+    take_input(ACT0, IN_F0, 0)
+    x_parts(PRE_F0, wu, xg[IN_F0])
+    gather_first(X1)
     inv, pre, slope = pre_backward(IN_B0, PRE_B0, 0)
     d_pre_backward(0, DH_B0, 0, pre, slope)
-    gather_relay(X1)
+    hidden_forward(IN_F0, PRE_F0, 1)
     inv_rows = by_row(inv)
     spread_full(0, normed_block(IN_B0, inv_rows))
+    gather_relay(X1)
+    branch_backward(B0, 0, IN_B0, 0, inv, inv_rows)
     branch_forward(F0, 1)
-    branch_backward(B0, 0, IN_B0, 0, inv, inv_rows)
     take_input(X1, IN_B1, 3)
     x_parts(PRE_B1, wu, xg[IN_B1])
+    sum_relay(B0)
     sum_relay(F0)
-    sum_relay(B0)
     spread_full(1, lambda c: dyb[0, :, block(c)])
+    grad = (sum_done(B0) + lines[0]).astype(bf16)
+    hand_on(1, jnp.where(sec == 0, loss_lines, grad), before, DY1)
     out = (sum_done(F0) + own_lines(xs.at[IN_F0])).astype(bf16)
     hand_on(0, jnp.where(sec == 7, first_lines, out), after, ACT1)
-    grad = (sum_done(B0) + lines[0]).astype(bf16)
-    hand_on(1, jnp.where(sec == 0, loss_lines, grad), before, DY1)
-
-    results_out(0, out.astype(f32))
-    results_out(1, grad.astype(f32))
+
     inv, pre, slope = pre_backward(IN_B1, PRE_B1, 1)
     inv_rows = by_row(inv)
+    results_out(1, grad.astype(f32))
+    results_out(0, out.astype(f32))
+    gather_relay(DY1)
+    gather_relay(ACT1)
     spread_full(2, normed_block(IN_B1, inv_rows))
-    gather_relay(ACT1)
-    gather_relay(DY1)
+    wait_bytes(gat.at[DY1, 0], pr.at[1])
+    take_grad(DY1, 1, 3)
+    x_parts(DH_B1, wd, dyb[1])
     wait_bytes(gat.at[ACT1, 0], pr.at[0])
     take_input(ACT1, IN_F1, 1)
     x_parts(PRE_F1, wu, xg[IN_F1])
-    wait_bytes(gat.at[DY1, 0], pr.at[1])
-    take_grad(DY1, 1, 3)
-    x_parts(DH_B1, wd, dyb[1])
+    d_pre_backward(1, DH_B1, 2, pre, slope)
     hidden_forward(IN_F1, PRE_F1, 3)
-    d_pre_backward(1, DH_B1, 2, pre, slope)
     spread_full(3, lambda c: dyb[1, :, block(c)])
+    branch_backward(B1, 2, IN_B1, 1, inv, inv_rows)
     branch_forward(F1, 3)
-    branch_backward(B1, 2, IN_B1, 1, inv, inv_rows)
-    gz[0] = jnp.concatenate([gpart[...], jnp.zeros((8 - BLOCKS, 128), f32)], axis=0)
-    z_first(gz.at[0], gz, gs.at[0], gr)
+    z_relay(gz, gs.at[0], gr)
+    sum_relay(B1)
     sum_relay(F1)
-    sum_relay(B1)
-    z_relay(gz, gs.at[0], gr)
     weight_grad(dpre, 0, upg, upg_hbm)
     results_in(0, out_ref, 0)
     results_in(1, grad_ref, 0)
-    results_out(3, sum_done(F1) + own_lines(xs.at[IN_F1]))
     results_out(2, sum_done(B1) + lines[1])
     z_near(gz, gr)
     z_far(gz, gr)
@@ -423,6 +444,7 @@
     gx[0] = total
     for d in (2, 1, 3):
         send(gx.at[0], gx.at[NX - d], gs.at[1], gr.at[7], at_x(d))
+    results_out(3, sum_done(F1) + own_lines(xs.at[IN_F1]))
 
     weight_grad(hid, 1, downg, downg_hbm)
     results_in(2, grad_ref, 1)
@@ -458,14 +480,16 @@
 
 def place(*refs):
     sources, targets, held, sem = refs[:5], refs[5:10], refs[10:15], refs[15]
-    loads, stores = [], []
-    for k in range(5):
-        loads.append(pltpu.make_async_copy(sources[k], held[k], sem.at[0, k]))
-        loads[k].start()
-    for k in range(5):
-        loads[k].wait()
-        stores.append(pltpu.make_async_copy(held[k], targets[k], sem.at[1, k]))
-        stores[k].start()
+    chunks = [(k, pl.ds(32 * n, 32)) for n in range(UNITS // 32) for k in (2, 3)]
+    moves = [(sources[k].at[0, part], held[k].at[0, part], targets[k].at[0, part]) for k, part in chunks]
+    moves += [(sources[k], held[k], targets[k]) for k in (0, 1, 4)]
+    loads = [pltpu.make_async_copy(move[0], move[1], sem.at[0, n]) for n, move in enumerate(moves)]
+    stores = [pltpu.make_async_copy(move[1], move[2], sem.at[1, n]) for n, move in enumerate(moves)]
+    for load in loads:
+        load.start()
+    for load, store in zip(loads, stores):
+        load.wait()
+        store.start()
     for store in stores:
         store.wait()
 
@@ -484,9 +508,17 @@
     results = pl.pallas_call(
         kernel,
         out_shape=shapes,
-        in_specs=[vmem] * 8 + [anywhere] * 2,
+        in_specs=[anywhere] * 10,
         out_specs=(vmem, vmem, anywhere, anywhere, vmem),
         scratch_shapes=[
+            pltpu.VMEM((1, 2, WIDTH), bf16),
+            pltpu.VMEM((1, 2, WIDTH), bf16),
+            pltpu.VMEM((2, 1, 2, WIDTH), bf16),
+            pltpu.VMEM((1, 2, WIDTH), bf16),
+            pltpu.VMEM((1, 2, WIDTH), bf16),
+            pltpu.VMEM((2, 8, ROWS), jnp.int32),
+            pltpu.VMEM((2, 8, ROWS), jnp.int32),
+            pltpu.VMEM((1, WIDTH), f32),
             pltpu.VMEM((NX, UNITS, SLICE), bf16),
             pltpu.VMEM((NX, UNITS, SLICE), bf16),
             pltpu.VMEM((NX, 64, 128), f32),
@@ -521,7 +553,7 @@
             pltpu.VMEM((4, ROWS, ROWS), bf16),
             pltpu.VMEM((NX, UNITS, SLICE), bf16),
             pltpu.VMEM((NX, UNITS, SLICE), bf16),
-            dma((2,)),
+            dma((10,)),
             dma((2,)),
             dma((2,)),
             dma((1,)),
@@ -558,7 +590,7 @@
         out_shape=shapes,
         in_specs=[anywhere] * 5,
         out_specs=(anywhere,) * 5,
-        scratch_shapes=[pltpu.VMEM(shape.shape, shape.dtype) for shape in shapes] + [dma((2, 5))],
+        scratch_shapes=[pltpu.VMEM(shape.shape, shape.dtype) for shape in shapes] + [dma((2, 16))],
     )(*results)
 
 

time: 98.3 us -> 96.5 us (0.982)
  the two profiles are of different devices: /device:TPU:16 before, /device:TPU:1 now
where the time goes in v4:
time: 96.5 us; the launch traced here: 96.3 us
  Pallas kernels  95.7 us (99%)
    pallas_call x1, Pallas kernels, on_device(): pl.pallas_call(kernel, out_shape=shapes, in_specs=[anywhere] * 10, out_sp...  93.2 us
    pallas_call x1, Pallas kernels, on_device(): pl.pallas_call(place, out_shape=shapes, in_specs=[anywhere] * 5, out_spec...  2.46 us

profile of v4, /device:TPU:1, one launch (start us, length us, event | category | flops | bytes accessed | tf_op | source)
XLA Modules:
  0.0 96.3 jit_solution(17597626507700609116)
XLA Ops:
  0.6 93.2 %shard_map.137 = (bf16[2,1,2,2560]{3,2,1,0:T(2,128)(2,1)}, bf16[2,1,2,2560]{3,2,1,0:T(2,128)(2,1)}, bf16[1,160,2560]{2,1,0:T(8,128)(2,1)}, bf16[1,160,2560]{2,1,0:T(8,128)(2,1)}, f32[1,2560]{1,0:T(1,128)}) custom-call(bf16[1,2,2560]{2,1,0:T(2,128)(2,1)} %act_hbm.1, bf16[1,2,2560]{2,1,0:T(2,128)(2,1)} %first_hbm.1, bf16[2,1,2,2560]{3,2,1,0:T(2,128)(2,1)} %stored_hbm.1, ...), custom_call_target="tpu_custom_call" | custom-call | tf_op jit(solution)/shard_map/pallas_call | solution.py:508
  93.8 2.5 %shard_map.138 = (bf16[2,1,2,2560]{3,2,1,0:T(2,128)(2,1)}, bf16[2,1,2,2560]{3,2,1,0:T(2,128)(2,1)}, bf16[1,160,2560]{2,1,0:T(8,128)(2,1)}, bf16[1,160,2560]{2,1,0:T(8,128)(2,1)}, f32[1,2560]{1,0:T(1,128)}) custom-call(bf16[2,1,2,2560]{3,2,1,0:T(2,128)(2,1)} %get-tuple-element.10.refs_0_, bf16[2,1,2,2560]{3,2,1,0:T(2,128)(2,1)} %get-tuple-element.11.refs_1_, ...), custom_call_target="tpu_custom_call" | custom-call | tf_op jit(solution)/shard_map/pallas_call | solution.py:588
